TPU v7x, 256 devices: a whole 4x4x8 slice. The times are simulated.
256 devices in a mesh: wedge: 64 (over x_lo, z, y), band: 4 (over x_hi, core).
Axes of the slice: x: 4 (x_hi: 2, x_lo: 2; x = x_hi * 2 + x_lo), y: 4, z: 8, core: 2. Of those that a mesh axis runs over, the one named last changes fastest.
Arguments:
- pulse_data: bfloat16 [2, 1024, 4096], P(None, 'wedge', 'band'), may hold values from -6 to 6
- phase_error: float32 [1024], P('wedge'), may hold values from -3.140625 to 3.140625
- steering: bfloat16 [2, 4096, 1024], P(None, 'wedge'), may hold values from -0.1875 to 0.1875
- kernel_bank: bfloat16 [8, 128, 4096], P(None, None, 'band'), may hold values from -0.25 to 0.25
- tile_offsets: int32 [64, 64, 4], replicated, may hold values from 0 to 7, as said below
- kernel_ids: int32 [64, 64, 4], replicated, may hold values from 0 to 7
- counts: int32 [64, 64], replicated, may hold values from 0 to 4, as said below
Outputs:
- focused: float32 [2, 4096, 4096], P(None, 'wedge', 'band')
- smoothed: float32 [2, 4096, 4096], P(None, 'wedge', 'band')
- phase_gradient: float32 [1024], P('wedge')
Inputs may be any that keep to these rules, and one draw needn't show every extreme that they name: counts[k, w] is the number of live slots of pulse block k at wedge w; 4 is reached. `tile_offsets`: the 4 tiles named for one pair are distinct; only the first counts[k, w] of them are used.
All inputs are finite; a program needn't handle non-finite values.
Results may differ from a plain program's by a relative error of at most 0.006.
Values may be sent and summed in bfloat16 or wider, within the bound.
A program may use at most 64 MiB of HBM per device.

v0:
```python
import math

import jax
import jax.numpy as jnp
from jax import lax
from jax.sharding import PartitionSpec as P

TILE = 128
MAXB = 4


EDGE_SOFTNESS = 0.05
STEP_SIZE = 0.25


def padded(cells, sides, width, closed):
    for axis, dim in sides:
        count = lax.axis_size(axis)
        ends = count if closed else count - 1
        head = lax.slice_in_dim(cells, 0, width, axis=dim)
        tail = lax.slice_in_dim(cells, cells.shape[dim] - width, cells.shape[dim], axis=dim)
        cells = jnp.concatenate(
            [
                lax.ppermute(tail, axis, [(i, (i + 1) % count) for i in range(ends)]),
                cells,
                lax.ppermute(head, axis, [((i + 1) % count, i) for i in range(ends)]),
            ],
            axis=dim,
        )
    return cells


def resample_pair(pulse_block, bank_band, offsets, kernels, count):
    pulse_rows = pulse_block.shape[1]
    radial_cells = bank_band.shape[2]
    pieces = [
        lax.dynamic_slice_in_dim(pulse_block, offsets[slot_index] * TILE, TILE, 2)
        for slot_index in range(MAXB)
    ]
    joined = jnp.reshape(jnp.concatenate(pieces, axis=2), (2 * pulse_rows, MAXB * TILE))
    live = (jnp.arange(MAXB) < count).astype(bank_band.dtype)
    chosen = jnp.take(bank_band, kernels, axis=0) * live[:, None, None]
    running = jnp.dot(
        joined, jnp.reshape(chosen, (MAXB * TILE, radial_cells)), preferred_element_type=jnp.float32
    )
    return jnp.reshape(running, (2, pulse_rows, radial_cells)).astype(jnp.bfloat16)


def edge_pull(difference):
    return difference / jnp.sqrt(
        jnp.sum(difference * difference, axis=0, keepdims=True) + EDGE_SOFTNESS
    )


def shards(pulse_data, phase_error, steering, kernel_bank, tile_offsets, kernel_ids, counts):
    pulse_rows = pulse_data.shape[1]
    radial_cells = kernel_bank.shape[2]
    azimuth_rows = steering.shape[1]
    wedges = lax.axis_size("wedge")
    band_count = lax.axis_size("band")
    wedge_index = lax.axis_index("wedge")
    band_index = lax.axis_index("band")
    pulse_total = pulse_rows * wedges
    cosine = jnp.cos(phase_error)[:, None]
    sine_part = jnp.sin(phase_error)[:, None]
    real_part = pulse_data[0].astype(jnp.float32)
    imag_part = pulse_data[1].astype(jnp.float32)
    corrected = jnp.stack(
        [real_part * cosine + imag_part * sine_part, imag_part * cosine - real_part * sine_part]
    ).astype(jnp.bfloat16)
    offsets_here = lax.dynamic_index_in_dim(tile_offsets, wedge_index, 1, keepdims=False)
    kernels_here = lax.dynamic_index_in_dim(kernel_ids, wedge_index, 1, keepdims=False)
    counts_here = lax.dynamic_index_in_dim(counts, wedge_index, 1, keepdims=False)
    empty = jnp.zeros((2, pulse_total, radial_cells), jnp.bfloat16)
    shard_piece = lax.all_gather(corrected, "wedge", axis=1, tiled=True)
    block_total = shard_piece.shape[1] // pulse_rows

    def one_block(slot_number, current):
        pulse_block = lax.dynamic_slice_in_dim(shard_piece, slot_number * pulse_rows, pulse_rows, 1)
        result = resample_pair(
            pulse_block,
            kernel_bank,
            offsets_here[slot_number],
            kernels_here[slot_number],
            counts_here[slot_number],
        )
        return lax.dynamic_update_slice_in_dim(current, result, slot_number * pulse_rows, 1)

    resampled = lax.fori_loop(0, block_total, one_block, empty)
    stacked_rows = jnp.reshape(resampled, (2 * pulse_total, radial_cells))
    left_real = jnp.concatenate([steering[0], -steering[1]], axis=1)
    left_imag = jnp.concatenate([steering[1], steering[0]], axis=1)
    focus_real = jnp.dot(left_real, stacked_rows, preferred_element_type=jnp.float32)
    focus_imag = jnp.dot(left_imag, stacked_rows, preferred_element_type=jnp.float32)
    squared = focus_real * focus_real + focus_imag * focus_imag
    cubed = jnp.stack([squared * focus_real, squared * focus_imag]).astype(jnp.bfloat16)
    cubed_rows = jnp.reshape(cubed, (2 * azimuth_rows, radial_cells))
    right_real = jnp.reshape(steering, (2 * azimuth_rows, pulse_total))
    right_imag = jnp.concatenate([steering[1], -steering[0]], axis=0)
    contract = (((0,), (0,)), ((), ()))
    back_real = lax.dot_general(
        right_real, cubed_rows, contract, preferred_element_type=jnp.float32
    )
    back_imag = lax.dot_general(
        right_imag, cubed_rows, contract, preferred_element_type=jnp.float32
    )
    partial_sum = jnp.sum(back_real * resampled[1] + back_imag * resampled[0], axis=1)
    owned = lax.psum_scatter(partial_sum, "wedge", scatter_dimension=0, tiled=True)
    summed_gradient = lax.psum(owned, "band")
    scale_factor = math.sqrt(pulse_total / (azimuth_rows * wedges * radial_cells * band_count))
    phase_gradient = scale_factor * summed_gradient
    focused = jnp.stack([focus_real, focus_imag])
    beside_all = padded(focused, (("wedge", 1),), 1, True)
    beside = padded(focused, (("band", 2),), 1, False)
    columns = jnp.arange(radial_cells)
    lower_valid = ((columns > 0) | (band_index > 0))[None, None, :]
    upper_valid = ((columns < radial_cells - 1) | (band_index < band_count - 1))[None, None, :]
    summed = edge_pull(focused - beside_all[:, :-2]) + edge_pull(focused - beside_all[:, 2:])
    summed = summed + jnp.where(lower_valid, edge_pull(focused - beside[:, :, :-2]), 0.0)
    summed = summed + jnp.where(upper_valid, edge_pull(focused - beside[:, :, 2:]), 0.0)
    smoothed = focused - STEP_SIZE * summed
    return (focused, smoothed, phase_gradient)


def solution(mesh):
    in_specs = (
        P(None, "wedge", "band"),
        P("wedge"),
        P(None, "wedge", None),
        P(None, None, "band"),
        P(),
        P(),
        P(),
    )
    out_specs = (P(None, "wedge", "band"), P(None, "wedge", "band"), P("wedge"))
    return jax.shard_map(shards, mesh=mesh, in_specs=in_specs, out_specs=out_specs, check_vma=False)
```

profile of v0, /device:TPU:1, one launch (start us, length us, event | category | flops | bytes accessed | tf_op | source)
XLA Modules:
  0.0 1005.5 jit_solution(593584477278989140)
XLA Ops:
  9.6 1.2 constant_dynamic-slice_fusion.6
  11.1 1.3 dynamic-slice
  13.2 1.0 slice_bitcast_fusion.2
  14.2 1.7 fusion.43
  15.9 258.6 %all-gather.2.cloned.1.call-done = bf16[2,1024,1024]{2,1,0:T(8,128)(2,1)} async-done(((bf16[2,16,1024]{2,1,0:T(8,128)(2,1)}), bf16[2,1024,1024]{2,1,0:T(8,128)(2,1)}) %all-gather.2.cloned.1.call-update) | async-done | bytes 4194320 | tf_op jit(solution)/shard_map/all_gather | solution.py:75
  274.5 2.5 broadcast_in_dim.52
  277.0 485.1 %while.16 = (s32[]{:T(128)}, bf16[2,1024,1024]{2,1,0:T(8,128)(2,1)}, s32[64,4]{0,1:T(4,128)S(1)}, bf16[2,1024,1024]{2,1,0:T(8,128)(2,1)}, s32[64,4]{1,0:T(8,128)...) while((s32[]{:T(128)}, ...), condition=%wide.region_1.2_spmd, body=%wide.region_0.1_spmd.sunk | while | flops 34767944 | bytes 5414551 | solution.py:89
  280.3 0.9 constant_dynamic-slice_fusion.11
  298.8 0.9 fusion.62
  310.6 0.9 constant_dynamic-slice_fusion.11
  340.9 0.9 constant_dynamic-slice_fusion.11
  359.4 0.9 fusion.62
  363.6 0.9 constant_dynamic-slice_fusion.11
  367.0 1.0 fusion.62
  374.6 1.0 fusion.62
  378.8 0.9 constant_dynamic-slice_fusion.11
  401.5 0.9 constant_dynamic-slice_fusion.11
  409.1 0.9 constant_dynamic-slice_fusion.11
  416.7 0.9 constant_dynamic-slice_fusion.11
  424.3 0.9 constant_dynamic-slice_fusion.11
  431.9 0.9 constant_dynamic-slice_fusion.11
  435.2 0.9 fusion.62
  439.4 0.9 constant_dynamic-slice_fusion.11
  447.0 0.9 constant_dynamic-slice_fusion.11
  462.2 0.9 constant_dynamic-slice_fusion.11
  469.8 0.9 constant_dynamic-slice_fusion.11
  484.9 0.9 constant_dynamic-slice_fusion.11
  492.5 0.9 constant_dynamic-slice_fusion.11
  507.7 1.0 constant_dynamic-slice_fusion.11
  515.3 0.9 constant_dynamic-slice_fusion.11
  530.5 0.9 constant_dynamic-slice_fusion.11
  568.3 0.9 constant_dynamic-slice_fusion.11
  571.6 0.9 fusion.62
  575.9 0.9 constant_dynamic-slice_fusion.11
  579.2 0.9 fusion.62
  598.6 0.9 constant_dynamic-slice_fusion.11
  606.2 0.9 constant_dynamic-slice_fusion.11
  621.4 0.9 constant_dynamic-slice_fusion.11
  636.5 0.9 constant_dynamic-slice_fusion.11
  644.1 0.9 constant_dynamic-slice_fusion.11
  651.7 1.0 constant_dynamic-slice_fusion.11
  655.1 0.9 fusion.62
  659.3 0.9 constant_dynamic-slice_fusion.11
  670.2 0.9 fusion.62
  674.5 0.9 constant_dynamic-slice_fusion.11
  677.8 1.0 fusion.62
  682.1 0.9 constant_dynamic-slice_fusion.11
  685.4 0.9 fusion.62
  697.2 0.9 constant_dynamic-slice_fusion.11
  700.6 0.9 fusion.62
  704.8 0.9 constant_dynamic-slice_fusion.11
  712.4 0.9 constant_dynamic-slice_fusion.11
  715.8 0.9 fusion.62
  723.3 0.9 fusion.62
  762.1 6.2 copy.21
  768.3 3.2 fusion.22
  773.6 1.2 copy-done.3
  774.8 1.1 fusion.13
  775.9 129.1 %all-reduce = f32[1024]{0:T(1024)S(1)} all-reduce(f32[1024]{0:T(1024)S(1)} %fusion.13), channel_id=2, replica_groups=mesh['wedge'=64,'band'=4] {'wedge'}, use_global_device_ids=true, to_apply=%region_7.8.clone | all-reduce | flops 1024 | bytes 8192
  905.1 78.0 %psum.7 = f32[16]{0:T(128)S(1)} all-reduce(f32[16]{0:T(128)S(1)} %dynamic-slice.1), channel_id=1, replica_groups=mesh['wedge'=64,'band'=4] {'band'}, use_global_device_ids=true, to_apply=%region_8.9 | all-reduce | flops 16 | bytes 128 | tf_op jit(solution)/shard_map/psum | solution.py:109
  983.1 4.8 collective-permute-start.2
  988.0 1.9 collective-permute-start.3
  990.0 5.7 collective-permute-start.1
  997.4 1.3 multiply_subtract_fusion
  (828 shorter events, 275.4 us)
Async XLA Ops:
  7.2 5.9 copy-start
  7.2 269.8 %copy-start.2 = (bf16[8,128,1024]{2,1,0:T(8,128)(2,1)S(1)}, bf16[8,128,1024]{2,1,0:T(8,128)(2,1)}, u32[]{:S(2)}) copy-start(bf16[8,128,1024]{2,1,0:T(8,128)(2,1)} %param.12) | copy-start | bytes 6291460
  7.2 267.3 %all-gather.2.cloned.1.call-start = ((), (), s32[]{:S(2)}) async-start(), calls=%async_computation | async-start | bytes 4259840 | tf_op jit(solution)/shard_map/all_gather | solution.py:75
  768.3 3.4 copy-start.1
  768.3 3.4 copy-start.7
  771.5 1.4 copy-start.6
  772.6 2.2 copy-start.3
  772.6 2.2 copy-start.5
  983.1 13.1 %collective-permute-start.2 = (f32[2,64,1]{2,1,0:T(8,128)S(1)}, f32[2,64,1]{2,1,0:T(8,128)S(1)}, u32[]{:S(2)}, u32[]{:S(2)}) collective-permute-start(f32[2,64,1]{2,1,0:T(8,128)S(1)} %get-tuple-element.249), channel_id=1, source_target_pairs={{0,1},{1,2},{2,3},{4,5},{5,6},{6,7},{8,9},{9,10},{10,11},{12,13},{... | collective-permute-start | bytes 1544 | tf_op jit(solution)/shard_map/ppermute | solution.py:24
  988.0 8.2 collective-permute-start.3
  989.9 6.8 collective-permute-start
  990.0 6.7 collective-permute-start.1
  997.1 1.6 copy-start.4
Sparse Core Ops, SparseCore 0:
  9.8 264.6 all-gather.1
where the time goes:
time: 1010 us
  waiting for transfers between devices  259 us (26%)
  local copies, waits for them, and re-layouts  207 us (20%)
  blocking collectives  207 us (20%)
  loops' own time  172 us (17%)
  other arithmetic  66.7 us (7%)
  matrix products  65.6 us (6%)
  between operations  14.9 us (1%)
  starting transfers between devices  12.6 us (1%)
    all_gather x1, waiting for transfers between devices, shards(): shard_piece = lax.all_gather(corrected, 'wedge', axis=1, tiled=True)  259 us
    another operation x1, loops' own time, shards(): resampled = lax.fori_loop(0, block_total, one_block, empty)  172 us
    unnamed x1, blocking collectives  129 us
    psum x1, blocking collectives, shards(): summed_gradient = lax.psum(owned, 'band')  78 us
    dynamic_slice x64, local copies, waits for them, and re-layouts, resample_pair(): lax.dynamic_slice_in_dim(pulse_block, offsets[slot_index] * TILE, TILE, 2)  59.8 us
    dot_general x64, matrix products, resample_pair(): jnp.dot(joined, jnp.reshape(chosen, (MAXB * TILE, radial_cells)), preferr...  59.7 us
    convert_element_type x64, other arithmetic, resample_pair(): live = (jnp.arange(MAXB) < count).astype(bank_band.dtype)  43.4 us
    dynamic_slice x64, local copies, waits for them, and re-layouts, one_block(): counts_here[slot_number]  41.5 us
  transfers between devices with their start and end apart: 5, of which 2 were waited for; matrix products, arithmetic and copies ran while one was open for 1% of the time, Pallas kernels for 0%

commit v1 on v0

v1 whole, which is shorter than its diff:
```python
import functools
import math

import jax
import jax.numpy as jnp
from jax import lax
from jax.experimental import pallas as pl
from jax.experimental.pallas import tpu as pltpu
from jax.sharding import PartitionSpec as P

TILE = 128
MAXB = 4
EDGE_SOFTNESS = 0.05
STEP_SIZE = 0.25
XN, ZN, YN, BN = 2, 8, 4, 4
MESH = pl.DeviceIdType.MESH
COPIES = 192


def kernel(scale, table, phase, pulses, steering, bank, focused_out, smoothed_out, gradient_out, *scratch):
    scratch = list(scratch)
    take = lambda n: [scratch.pop(0) for _ in range(n)]
    own0, pair0, own1 = take(ZN), take(ZN), take(ZN)
    column1 = take(ZN)
    y_send, y_got = take(ZN), take(ZN)
    x_send, x_got = take(ZN), take(ZN)
    lhs, resampled, bank_v, steer_v, image, smooth = take(6)
    rows_send, rows_got, cols_send, cols_got = take(4)
    part_one, got_one, part_two, got_two = take(4)
    send_sem, recv_sem, load_sem = take(3)

    w = lax.axis_index("wedge")
    b = lax.axis_index("band")
    x, z, y = w // (ZN * YN), lax.rem(w // YN, ZN), lax.rem(w, YN)

    def at(dx, dz, dy):
        return lax.rem(x + dx, XN) * (ZN * YN) + lax.rem(z + dz, ZN) * YN + lax.rem(y + dy, YN)

    loads = [
        pltpu.make_async_copy(bank, bank_v, load_sem.at[0]),
        pltpu.make_async_copy(steering, steer_v, load_sem.at[1]),
    ]
    for load in loads:
        load.start()

    greeted = [(at(0, dz, 0), b) for dz in range(1, ZN)]
    plane = [
        (dx, dy, db) for db in range(BN) for dx in range(XN) for dy in range(YN) if (dx, dy, db) != (0, 0, 0)
    ]
    greeted += [(at(dx, 0, dy), lax.rem(b + db, BN)) for dx, dy, db in plane]
    wedges = XN * ZN * YN
    after, before = lax.rem(w + 1, wedges), lax.rem(w + wedges - 1, wedges)
    greeted += [(after, b), (before, b)]
    barrier = pltpu.get_barrier_semaphore()
    for device in greeted:
        pl.semaphore_signal(barrier, inc=1, device_id=device, device_id_type=MESH)

    square = lax.broadcasted_iota(jnp.int32, (16, 16), 0) == lax.broadcasted_iota(jnp.int32, (16, 16), 1)
    angle = jnp.sum(jnp.where(square, phase[...], 0.0), axis=1, keepdims=True)
    cosine, sine = jnp.cos(angle), jnp.sin(angle)
    real, imag = pulses[0].astype(jnp.float32), pulses[1].astype(jnp.float32)
    fixed0 = (real * cosine + imag * sine).astype(jnp.bfloat16)
    fixed1 = (imag * cosine - real * sine).astype(jnp.bfloat16)
    for t in range(8):
        own0[0][t] = fixed0[:, t * TILE : (t + 1) * TILE]
        own1[0][t] = fixed1[:, t * TILE : (t + 1) * TILE]

    pl.semaphore_wait(barrier, len(greeted))

    started = []

    def copy(src, dst, device):
        index = len(started)
        made = pltpu.make_async_remote_copy(
            src, dst, send_sem.at[index], recv_sem.at[index], device_id=device, device_id_type=MESH
        )
        made.start()
        started.append(made)
        return made

    ring = {}

    def send_ring(stream, bufs, d):
        up, down = (at(0, 1, 0), b), (at(0, ZN - 1, 0), b)
        src_up, dst_up = bufs[(1 - d) % ZN], bufs[-d % ZN]
        src_down, dst_down = bufs[d - 1], bufs[d]
        if d == ZN // 2:
            low = (slice(None),) * (len(dst_up.shape) - 4) + (pl.ds(0, 4),)
            high = (slice(None),) * (len(dst_up.shape) - 4) + (pl.ds(4, 4),)
            if len(dst_up.shape) == 3:
                low, high = pl.ds(0, 4), pl.ds(4, 4)
            else:
                low, high = (slice(None), pl.ds(0, 4)), (slice(None), pl.ds(4, 4))
            src_up, dst_up = src_up.at[low], dst_up.at[low]
            src_down, dst_down = src_down.at[high], dst_down.at[high]
        ring[stream, d] = (copy(src_up, dst_up, up), copy(src_down, dst_down, down))

    def take_ring(stream, bufs, d):
        for made in ring[stream, d]:
            made.wait_recv()
        if d < ZN // 2:
            send_ring(stream, bufs, d + 1)

    def block_at(e, dx, dy):
        return at(dx, e, dy)

    def pick(which, k, j):
        return table[which * (wedges * MAXB) + k * MAXB + j]

    y_copies, x_copies = {}, {}

    def share(e):
        for dx, bufs in ((0, own0), (1, pair0)):
            k = block_at(e, dx, 0)
            for dy in range(1, YN):
                for j in range(MAXB):
                    y_send[e][dy - 1, dx, j] = bufs[e][pick(dy, k, j)]
        y_copies[e] = [
            copy(y_send[e].at[dy - 1], y_got[e].at[YN - dy - 1], (at(0, 0, dy), b)) for dy in range(1, YN)
        ]
        for dy in range(YN):
            k = block_at(e, 0, dy)
            for j in range(MAXB):
                t = pick(4, k, j)
                x_send[e][dy, j] = own1[e][t] if dy == 0 else column1[e][dy - 1, t]
        x_copies[e] = [copy(x_send[e], x_got[e], (at(1, 0, 0), b))]

    def place(row, k, load):
        tiles = [load(j).astype(jnp.float32) for j in range(MAXB)]
        names = [pick(5, k, j) for j in range(MAXB)]
        row = pl.multiple_of(row, 16)
        for m in range(8):
            total = jnp.zeros((16, TILE), jnp.float32)
            for j in range(MAXB):
                total = total + jnp.where(names[j] == m, tiles[j], 0.0)
            lhs[pl.ds(row, 16), m * TILE : (m + 1) * TILE] = total.astype(jnp.bfloat16)

    def process(es):
        for index, e in enumerate(es):
            for made in y_copies[e] + x_copies[e]:
                made.wait_recv()

            def row_of(q, dx, dy, index=index):
                return index * 256 + q * 128 + lax.rem(x + dx, XN) * 64 + lax.rem(y + dy, YN) * 16

            for dx, bufs in ((0, own0), (1, pair0)):
                k = block_at(e, dx, 0)
                place(row_of(0, dx, 0), k, lambda j: bufs[e][pick(0, k, j)])
            k = block_at(e, 0, 0)
            place(row_of(1, 0, 0), k, lambda j: own1[e][pick(0, k, j)])

            @pl.loop(1, YN)
            def _(dy, e=e, row_of=row_of):
                for dx in range(XN):
                    k = block_at(e, dx, dy)
                    place(row_of(0, dx, dy), k, lambda j: y_got[e][dy - 1, dx, j])
                k = block_at(e, 0, dy)
                place(row_of(1, 0, dy), k, lambda j: column1[e][dy - 1, pick(0, k, j)])

            @pl.loop(0, YN)
            def _(dy, e=e, row_of=row_of):
                k = block_at(e, 1, dy)
                place(row_of(1, 1, dy), k, lambda j: x_got[e][dy, j])

        @pl.loop(0, 4)
        def _(n):
            columns = pl.ds(pl.multiple_of(n * 256, 256), 256)
            rows = 256 * len(es)
            got = jnp.dot(lhs[0:rows, :], bank_v[:, columns], preferred_element_type=jnp.float32)
            got = got.astype(jnp.bfloat16)
            for index, e in enumerate(es):
                for q in range(2):
                    for xa in range(XN):
                        start = q * 1024 + xa * 512 + lax.rem(z + e, ZN) * 64
                        here = index * 256 + q * 128 + xa * 64
                        resampled[pl.ds(pl.multiple_of(start, 64), 64), columns] = got[here : here + 64]

    def slices(d):
        return [0] if d == 0 else [4] if d == 4 else [d, ZN - d]

    first_x = copy(own0[0], pair0[0], (at(1, 0, 0), b))
    send_ring("own0", own0, 1)
    first_y = [copy(own1[0], column1[0].at[YN - dy - 1], (at(0, 0, dy), b)) for dy in range(1, YN)]
    send_ring("own1", own1, 1)
    for turn in range(1, 6):
        if turn <= 4:
            take_ring("own0", own0, turn)
            take_ring("own1", own1, turn)
        if turn == 1:
            first_x.wait_recv()
            send_ring("pair0", pair0, 1)
            for made in first_y:
                made.wait_recv()
            send_ring("column1", column1, 1)
        else:
            take_ring("pair0", pair0, turn - 1)
            take_ring("column1", column1, turn - 1)
        for e in slices(turn - 1):
            share(e)
        if turn == 3:
            for load in loads:
                load.wait()
        if turn >= 3:
            process(slices(turn - 3))
    process(slices(3))
    process(slices(4))

    steer = steer_v[...]
    for n in range(4):
        columns = slice(n * 256, (n + 1) * 256)
        by_real = jnp.dot(steer, resampled[0:1024, columns], preferred_element_type=jnp.float32)
        by_imag = jnp.dot(steer, resampled[1024:2048, columns], preferred_element_type=jnp.float32)
        image[0, :, columns] = by_real[:64] - by_imag[64:]
        image[1, :, columns] = by_imag[:64] + by_real[64:]
    stores = [pltpu.make_async_copy(image, focused_out, load_sem.at[2])]
    stores[0].start()

    rows_send[0] = image[:, 0, :]
    rows_send[1] = image[:, 63, :]
    eye = lax.broadcasted_iota(jnp.int32, (128, 128), 0) == lax.broadcasted_iota(jnp.int32, (128, 128), 1)
    for side, column in ((0, 0), (1, 1023)):
        values = jnp.concatenate([image[0, :, column : column + 1], image[1, :, column : column + 1]], axis=0)
        cols_send[side] = jnp.sum(jnp.where(eye, values, 0.0), axis=0, keepdims=True)
    edge = [
        copy(rows_send.at[0], rows_got.at[1], (before, b)),
        copy(rows_send.at[1], rows_got.at[0], (after, b)),
        copy(cols_send.at[0], cols_got.at[1], (w, lax.rem(b + BN - 1, BN))),
        copy(cols_send.at[1], cols_got.at[0], (w, lax.rem(b + 1, BN))),
    ]

    squared = image[0] * image[0] + image[1] * image[1]
    cubed = jnp.concatenate([squared * image[0], squared * image[1]], axis=0).astype(jnp.bfloat16)
    across = (((1,), (1,)), ((), ()))
    for n in range(8):
        pulses_here = slice(n * 128, (n + 1) * 128)
        late = slice(1024 + n * 128, 1024 + (n + 1) * 128)
        by0 = lax.dot_general(cubed, resampled[pulses_here, :], across, preferred_element_type=jnp.float32)
        by1 = lax.dot_general(cubed, resampled[late, :], across, preferred_element_type=jnp.float32)
        s0 = steer_v[0:64, pulses_here].astype(jnp.float32)
        s1 = steer_v[64:128, pulses_here].astype(jnp.float32)
        terms = s0 * (by1[:64] - by0[64:]) + s1 * (by1[64:] + by0[:64])
        part_one[n] = jnp.sum(terms, axis=0, keepdims=True)
    one = [copy(part_one, got_one.at[ZN - dz - 1], (at(0, dz, 0), b)) for dz in range(1, ZN)]

    for made in edge:
        made.wait_recv()
    row = lax.broadcasted_iota(jnp.int32, (64, 1024), 0)
    col = lax.broadcasted_iota(jnp.int32, (64, 1024), 1)

    def pull(d0, d1):
        inverse = lax.rsqrt(d0 * d0 + d1 * d1 + EDGE_SOFTNESS)
        return d0 * inverse, d1 * inverse

    f = [image[0], image[1]]
    above = [jnp.where(row == 0, rows_got[0, i : i + 1], pltpu.roll(f[i], 1, 0)) for i in range(2)]
    up = pull(f[0] - above[0], f[1] - above[1])
    below = [jnp.where(row == 63, rows_got[1, i : i + 1], pltpu.roll(f[i], 63, 0)) for i in range(2)]
    down = pull(f[0] - below[0], f[1] - below[1])
    beside = []
    for side in range(2):
        values = jnp.sum(jnp.where(eye, cols_got[side], 0.0), axis=1, keepdims=True)
        beside.append([values[:64], values[64:]])
    left = [jnp.where(col == 0, beside[0][i], pltpu.roll(f[i], 1, 1)) for i in range(2)]
    inward = pull(f[0] - left[0], f[1] - left[1])
    right = [jnp.where(col == 1023, beside[1][i], pltpu.roll(f[i], 1023, 1)) for i in range(2)]
    outward = pull(f[0] - right[0], f[1] - right[1])
    lower = (col > 0) | (b > 0)
    upper = (col < 1023) | (b < BN - 1)
    for i in range(2):
        total = up[i] + down[i] + jnp.where(lower, inward[i], 0.0) + jnp.where(upper, outward[i], 0.0)
        smooth[i] = f[i] - STEP_SIZE * total
    stores.append(pltpu.make_async_copy(smooth, smoothed_out, load_sem.at[3]))
    stores[1].start()

    for made in one:
        made.wait_recv()
    total = part_one[...]
    for i in range(ZN - 1):
        total = total + got_one[i]
    part_two[...] = total
    two = []
    for i, (dx, dy, db) in enumerate(plane):
        other = plane.index(((XN - dx) % XN, (YN - dy) % YN, (BN - db) % BN))
        source = part_two.at[lax.rem(x + dx, XN) * 4 + z // 2]
        two.append(copy(source, got_two.at[other], (at(dx, 0, dy), lax.rem(b + db, BN))))
    for made in two:
        made.wait_recv()
    row_sum = part_two[x * 4 + z // 2]
    for i in range(len(plane)):
        row_sum = row_sum + got_two[i]
    offset = lax.rem(z, 2) * 64 + y * 16
    gradient_out[...] = pltpu.roll(jnp.broadcast_to(row_sum, (8, TILE)), lax.rem(TILE - offset, TILE), 1)[0:1, :16] * scale

    for made in started:
        made.wait_send()
    for store in stores:
        store.wait()


def shards(pulse_data, phase_error, steering, kernel_bank, tile_offsets, kernel_ids, counts):
    w = lax.axis_index("wedge")
    x, z, y = w // (ZN * YN), (w // YN) % ZN, w % YN
    near = [w] + [x * 32 + z * 4 + (y + dy) % YN for dy in range(1, YN)] + [(w + 32) % 64]
    rows = [lax.dynamic_index_in_dim(tile_offsets, k, 1, keepdims=False) for k in near]
    ids = lax.dynamic_index_in_dim(kernel_ids, w, 1, keepdims=False)
    live = lax.dynamic_index_in_dim(counts, w, 1, keepdims=False)
    ids = jnp.where(jnp.arange(MAXB)[None, :] < live[:, None], ids, 8)
    table = jnp.reshape(jnp.stack(rows + [ids]), (-1,))
    bf, f32 = jnp.bfloat16, jnp.float32
    block = pltpu.VMEM((8, 16, TILE), bf)
    scratch = [block] * 24
    scratch += [pltpu.VMEM((3, 8, 16, TILE), bf)] * 8
    scratch += [pltpu.VMEM((3, 2, 4, 16, TILE), bf)] * 16
    scratch += [pltpu.VMEM((4, 4, 16, TILE), bf)] * 16
    scratch += [
        pltpu.VMEM((512, 1024), bf),
        pltpu.VMEM((2048, 1024), bf),
        pltpu.VMEM((1024, 1024), bf),
        pltpu.VMEM((128, 1024), bf),
        pltpu.VMEM((2, 64, 1024), f32),
        pltpu.VMEM((2, 64, 1024), f32),
        pltpu.VMEM((2, 2, 1024), f32),
        pltpu.VMEM((2, 2, 1024), f32),
        pltpu.VMEM((2, 1, TILE), f32),
        pltpu.VMEM((2, 1, TILE), f32),
        pltpu.VMEM((8, 1, TILE), f32),
        pltpu.VMEM((7, 8, 1, TILE), f32),
        pltpu.VMEM((8, 1, TILE), f32),
        pltpu.VMEM((31, 1, TILE), f32),
        pltpu.SemaphoreType.DMA((COPIES,)),
        pltpu.SemaphoreType.DMA((COPIES,)),
        pltpu.SemaphoreType.DMA((4,)),
    ]
    scale = math.sqrt(1024 / (4096 * 4096))
    image = jax.ShapeDtypeStruct((2, 64, 1024), f32)
    vmem = pl.BlockSpec(memory_space=pltpu.VMEM)
    anywhere = pl.BlockSpec(memory_space=pl.ANY)
    focused, smoothed, gradient = pl.pallas_call(
        functools.partial(kernel, scale),
        out_shape=(image, image, jax.ShapeDtypeStruct((1, 16), f32)),
        in_specs=[pl.BlockSpec(memory_space=pltpu.SMEM), vmem, vmem, anywhere, anywhere],
        out_specs=(anywhere, anywhere, vmem),
        scratch_shapes=scratch,
        compiler_params=pltpu.CompilerParams(
            collective_id=0, has_side_effects=True, vmem_limit_bytes=40 << 20
        ),
    )(
        table,
        jnp.reshape(phase_error, (1, 16)),
        pulse_data,
        jnp.reshape(steering, (128, 1024)),
        jnp.reshape(kernel_bank, (1024, 1024)),
    )
    return focused, smoothed, jnp.reshape(gradient, (16,))


def solution(mesh):
    in_specs = (
        P(None, "wedge", "band"),
        P("wedge"),
        P(None, "wedge", None),
        P(None, None, "band"),
        P(),
        P(),
        P(),
    )
    out_specs = (P(None, "wedge", "band"), P(None, "wedge", "band"), P("wedge"))
    return jax.shard_map(shards, mesh=mesh, in_specs=in_specs, out_specs=out_specs, check_vma=False)
```

time: 1010 us -> 64.3 us (0.06)
  waiting for transfers between devices: 259 us -> 0 us
  blocking collectives: 207 us -> 0 us
  local copies, waits for them, and re-layouts: 207 us -> 5.72 us
  loops' own time: 172 us -> 0 us
  other arithmetic: 66.7 us -> 0.01 us
  matrix products: 65.6 us -> 0 us
  Pallas kernels: 0 us -> 57.6 us
  between operations: 14.9 us -> 0.87 us
  starting transfers between devices: 12.6 us -> 0 us
    all_gather x1 -> x0, waiting for transfers between devices: 259 us -> none  [shards(): shard_piece = lax.all_gather(corrected, 'wedge', axis=1, tiled=True)]
    another operation x1 -> x0, loops' own time: 172 us -> none  [shards(): resampled = lax.fori_loop(0, block_total, one_block, empty)]
    unnamed x1 -> x0, blocking collectives: 129 us -> none
    dynamic_slice x196 -> x8, local copies, waits for them, and re-layouts: 107 us -> 2.7 us  [the longest x6 2.41 us: shards(): lax.dynamic_index_in_dim(tile_offsets, k, 1, keepdims=False)]
    psum x1 -> x0, blocking collectives: 78 us -> none  [shards(): summed_gradient = lax.psum(owned, 'band')]
    dot_general x68 -> x0, matrix products: 65.6 us -> none  [the longest x64 59.7 us: resample_pair(): jnp.dot(joined, jnp.reshape(chosen, (MAXB * TILE, radial_cells)), preferr...]
    pallas_call x0 -> x1, Pallas kernels: none -> 57.6 us  [shards(): pl.pallas_call(functools.partial(kernel, scale), out_shape=(image, image,...]
    convert_element_type x65 -> x0, other arithmetic: 43.4 us -> none  [the longest x64 43.4 us: resample_pair(): live = (jnp.arange(MAXB) < count).astype(bank_band.dtype)]
  transfers between devices with their start and end apart: 5 -> 0, of which waited for: 2 -> 0; matrix products, arithmetic and copies ran while one was open for 1% -> 0% of each run, Pallas kernels for 0% -> 0%
where the time goes in v1:
time: 64.3 us; the launch traced here: 64.2 us
  Pallas kernels  57.6 us (90%)
  local copies, waits for them, and re-layouts  5.72 us (9%)
  between operations  0.87 us (1%)
    pallas_call x1, Pallas kernels, shards(): pl.pallas_call(functools.partial(kernel, scale), out_shape=(image, image,...  57.6 us
    unnamed x18, local copies, waits for them, and re-layouts  2.75 us
    dynamic_slice x6, local copies, waits for them, and re-layouts, shards(): lax.dynamic_index_in_dim(tile_offsets, k, 1, keepdims=False)  2.41 us

profile of v1, /device:TPU:1, one launch (start us, length us, event | category | flops | bytes accessed | tf_op | source)
XLA Modules:
  0.0 64.2 jit_solution(3868932345084309387)
XLA Ops:
  0.6 0.0 copy-start
  0.6 0.0 copy-start.1
  0.7 0.0 copy-start.2
  0.7 0.0 copy-start.4
  0.7 0.0 copy-start.3
  0.8 0.6 copy-done
  1.4 0.2 dynamic-slice_reduce_fusion
  1.6 1.9 %constant_dynamic-slice_fusion.1 = (s32[64,1,4]{1,2,0:T(4,128)S(1)}, s32[64,1,4]{1,2,0:T(4,128)S(1)}, s32[64,1,4]{1,2,0:T(4,128)S(1)}, s32[64,1,4]{1,2,0:T(4,128...) fusion(s32[64,64,4]{1,2,0:T(4,128)} %param.11, s32[]{:T(128)S(6)} %select_n.76, s32[]{:T(128)S(6)} %select_n.72, ...), kind=kLoop, calls=%fused_computation.10 | loop fusion | bytes 12308 | tf_op jit(solution)/shard_map/jit(dynamic_index_in_dim)/dynamic_slice | solution.py:304
  3.4 0.1 copy.14
  3.5 0.1 copy.12
  3.6 0.1 copy.11
  3.8 0.1 copy.10
  3.9 0.1 copy.13
  4.0 0.1 copy.15
  4.2 0.1 copy.16
  4.3 0.1 reshape.74.table
  4.5 0.0 copy-done.1
  4.5 0.0 copy-done.2
  4.5 0.0 copy-done.4
  4.5 0.0 copy-done.3
  4.5 57.6 %shard_map.94 = (f32[2,64,1024]{2,1,0:T(8,128)S(1)}, f32[2,64,1024]{2,1,0:T(8,128)S(1)}, f32[1,16]{1,0:T(1,128)S(1)}) custom-call(s32[1536]{0:T(1024)S(1)} %reshape.74.table, f32[1,16]{1,0:T(1,128)S(1)} %bitcast.20, bf16[2,16,1024]{2,1,0:T(8,128)(2,1)S(1)} %copy-done.3, bf16[128,1024]{1,0:T(8,128)(2,1)S(1)} %bitcast.19, bf16[1024,1024]{1,0:T(8,128)(2,1)S(1)} %bitcast.18), custom_call_target="tpu_custom_call" | custom-call | tf_op jit(solution)/shard_map/pallas_call | solution.py:338
  62.1 0.8 %copy.25 = f32[2,64,1024]{2,1,0:T(8,128)} copy(f32[2,64,1024]{2,1,0:T(8,128)S(1)} %get-tuple-element.18) | data formatting | bytes 1048576
  62.9 0.8 %copy.26 = f32[2,64,1024]{2,1,0:T(8,128)} copy(f32[2,64,1024]{2,1,0:T(8,128)S(1)} %get-tuple-element.19) | data formatting | bytes 1048576
  63.7 0.5 copy.27
  (6 shorter events, 0.0 us)
Async XLA Ops:
  0.6 0.8 %copy-start = (s32[64,64]{1,0:T(8,128)S(1)}, s32[64,64]{1,0:T(8,128)}, u32[]{:S(2)}) copy-start(s32[64,64]{1,0:T(8,128)} %param.13) | copy-start | bytes 49156
  0.6 3.8 %copy-start.1 = (bf16[8,128,1024]{2,1,0:T(8,128)(2,1)S(1)}, bf16[8,128,1024]{2,1,0:T(8,128)(2,1)}, u32[]{:S(2)}) copy-start(bf16[8,128,1024]{2,1,0:T(8,128)(2,1)} %param.10) | copy-start | bytes 6291460
  0.7 3.8 %copy-start.2 = (bf16[2,64,1024]{2,1,0:T(8,128)(2,1)S(1)}, bf16[2,64,1024]{2,1,0:T(8,128)(2,1)}, u32[]{:S(2)}) copy-start(bf16[2,64,1024]{2,1,0:T(8,128)(2,1)} %param.9) | copy-start | bytes 786436
  0.7 3.8 %copy-start.4 = (f32[16]{0:T(128)S(1)}, f32[16]{0:T(128)}, u32[]{:S(2)}) copy-start(f32[16]{0:T(128)} %param.8) | copy-start | bytes 196
  0.7 3.8 %copy-start.3 = (bf16[2,16,1024]{2,1,0:T(8,128)(2,1)S(1)}, bf16[2,16,1024]{2,1,0:T(8,128)(2,1)}, u32[]{:S(2)}) copy-start(bf16[2,16,1024]{2,1,0:T(8,128)(2,1)} %pulses.1) | copy-start | bytes 196612

commit v2 on v1

--- a/solution.py
+++ b/solution.py
@@ -17,7 +17,7 @@
 COPIES = 192
 
 
-def kernel(scale, table, phase, pulses, steering, bank, focused_out, smoothed_out, gradient_out, *scratch):
+def kernel(scale, offsets_in, ids_in, counts_in, phase_in, pulses_in, steering, bank, focused_out, smoothed_out, gradient_out, *scratch):
     scratch = list(scratch)
     take = lambda n: [scratch.pop(0) for _ in range(n)]
     own0, pair0, own1 = take(ZN), take(ZN), take(ZN)
@@ -27,6 +27,7 @@
     lhs, resampled, bank_v, steer_v, image, smooth = take(6)
     rows_send, rows_got, cols_send, cols_got = take(4)
     part_one, got_one, part_two, got_two = take(4)
+    offsets, ids, counts, phase, pulses, table_v, table = take(7)
     send_sem, recv_sem, load_sem = take(3)
 
     w = lax.axis_index("wedge")
@@ -36,26 +37,27 @@
     def at(dx, dz, dy):
         return lax.rem(x + dx, XN) * (ZN * YN) + lax.rem(z + dz, ZN) * YN + lax.rem(y + dy, YN)
 
-    loads = [
-        pltpu.make_async_copy(bank, bank_v, load_sem.at[0]),
-        pltpu.make_async_copy(steering, steer_v, load_sem.at[1]),
-    ]
-    for load in loads:
-        load.start()
-
-    greeted = [(at(0, dz, 0), b) for dz in range(1, ZN)]
-    plane = [
-        (dx, dy, db) for db in range(BN) for dx in range(XN) for dy in range(YN) if (dx, dy, db) != (0, 0, 0)
-    ]
-    greeted += [(at(dx, 0, dy), lax.rem(b + db, BN)) for dx, dy, db in plane]
+    def load(src, dst, n):
+        made = pltpu.make_async_copy(src, dst, load_sem.at[n])
+        made.start()
+        return made
+
+    first_loads = [load(pulses_in, pulses, 4), load(phase_in, phase, 5)]
+    index_loads = [load(offsets_in, offsets, 6), load(ids_in, ids, 7), load(counts_in, counts, 8)]
+    loads = [load(bank, bank_v, 0), load(steering, steer_v, 1)]
+
     wedges = XN * ZN * YN
     after, before = lax.rem(w + 1, wedges), lax.rem(w + wedges - 1, wedges)
-    greeted += [(after, b), (before, b)]
+    greeted = [(at(0, 1, 0), b), (at(0, ZN - 1, 0), b), (at(1, 0, 0), b)]
+    greeted += [(at(0, 0, dy), b) for dy in range(1, YN)]
+    greeted += [(w, lax.rem(b + db, BN)) for db in range(1, BN)]
     barrier = pltpu.get_barrier_semaphore()
     for device in greeted:
         pl.semaphore_signal(barrier, inc=1, device_id=device, device_id_type=MESH)
 
     square = lax.broadcasted_iota(jnp.int32, (16, 16), 0) == lax.broadcasted_iota(jnp.int32, (16, 16), 1)
+    for made in first_loads:
+        made.wait()
     angle = jnp.sum(jnp.where(square, phase[...], 0.0), axis=1, keepdims=True)
     cosine, sine = jnp.cos(angle), jnp.sin(angle)
     real, imag = pulses[0].astype(jnp.float32), pulses[1].astype(jnp.float32)
@@ -105,7 +107,7 @@
         return at(dx, e, dy)
 
     def pick(which, k, j):
-        return table[which * (wedges * MAXB) + k * MAXB + j]
+        return table[which, k * MAXB + j]
 
     y_copies, x_copies = {}, {}
 
@@ -127,7 +129,7 @@
 
     def place(row, k, load):
         tiles = [load(j).astype(jnp.float32) for j in range(MAXB)]
-        names = [pick(5, k, j) for j in range(MAXB)]
+        names = [jnp.where(j < table[6, k], pick(5, k, j), 8) for j in range(MAXB)]
         row = pl.multiple_of(row, 16)
         for m in range(8):
             total = jnp.zeros((16, TILE), jnp.float32)
@@ -182,6 +184,27 @@
     send_ring("own0", own0, 1)
     first_y = [copy(own1[0], column1[0].at[YN - dy - 1], (at(0, 0, dy), b)) for dy in range(1, YN)]
     send_ring("own1", own1, 1)
+
+    for made in index_loads:
+        made.wait()
+    near = [w] + [at(0, 0, dy) for dy in range(1, YN)] + [at(1, 0, 0), w, w]
+    kind = lax.broadcasted_iota(jnp.int32, (8, wedges), 0)
+    lane = lax.broadcasted_iota(jnp.int32, (8, wedges), 1)
+    wanted = jnp.zeros((8, wedges), jnp.int32)
+    for n, wedge in enumerate(near):
+        wanted = jnp.where(kind == n, wedge, wanted)
+    chosen = jnp.where(lane == wanted, 1.0, 0.0).astype(jnp.bfloat16)
+    across = (((1,), (1,)), ((), ()))
+
+    def choose(ref, rows):
+        values = jnp.reshape(ref[...], (rows, wedges)).astype(jnp.float32).astype(jnp.bfloat16)
+        return lax.dot_general(chosen, values, across, preferred_element_type=jnp.float32).astype(jnp.int32)
+
+    row = lax.broadcasted_iota(jnp.int32, (8, wedges * MAXB), 0)
+    picked = jnp.where(row == 5, choose(ids, wedges * MAXB), choose(offsets, wedges * MAXB))
+    table_v[...] = jnp.clip(picked, 0, 7)
+    table_v[6:7, 0:wedges] = choose(counts, wedges)[6:7]
+    load(table_v, table, 9).wait()
     for turn in range(1, 6):
         if turn <= 4:
             take_ring("own0", own0, turn)
@@ -197,12 +220,11 @@
             take_ring("column1", column1, turn - 1)
         for e in slices(turn - 1):
             share(e)
-        if turn == 3:
-            for load in loads:
-                load.wait()
-        if turn >= 3:
-            process(slices(turn - 3))
-    process(slices(3))
+        if turn == 2:
+            for made in loads:
+                made.wait()
+        if turn >= 2:
+            process(slices(turn - 2))
     process(slices(4))
 
     steer = steer_v[...]
@@ -230,7 +252,6 @@
 
     squared = image[0] * image[0] + image[1] * image[1]
     cubed = jnp.concatenate([squared * image[0], squared * image[1]], axis=0).astype(jnp.bfloat16)
-    across = (((1,), (1,)), ((), ()))
     for n in range(8):
         pulses_here = slice(n * 128, (n + 1) * 128)
         late = slice(1024 + n * 128, 1024 + (n + 1) * 128)
@@ -240,7 +261,12 @@
         s1 = steer_v[64:128, pulses_here].astype(jnp.float32)
         terms = s0 * (by1[:64] - by0[64:]) + s1 * (by1[64:] + by0[:64])
         part_one[n] = jnp.sum(terms, axis=0, keepdims=True)
-    one = [copy(part_one, got_one.at[ZN - dz - 1], (at(0, dz, 0), b)) for dz in range(1, ZN)]
+    core, half = lax.rem(b, 2), b // 2
+    first_group = [(dz, dc) for dc in range(2) for dz in range(ZN) if (dz, dc) != (0, 0)]
+    one = []
+    for dz, dc in first_group:
+        other = first_group.index(((ZN - dz) % ZN, dc))
+        one.append(copy(part_one, got_one.at[other], (at(0, dz, 0), half * 2 + lax.rem(core + dc, 2))))
 
     for made in edge:
         made.wait_recv()
@@ -275,21 +301,23 @@
     for made in one:
         made.wait_recv()
     total = part_one[...]
-    for i in range(ZN - 1):
+    for i in range(len(first_group)):
         total = total + got_one[i]
     part_two[...] = total
+    second_group = [(dh, dx, dy) for dh in range(2) for dx in range(XN) for dy in range(YN) if (dh, dx, dy) != (0, 0, 0)]
     two = []
-    for i, (dx, dy, db) in enumerate(plane):
-        other = plane.index(((XN - dx) % XN, (YN - dy) % YN, (BN - db) % BN))
+    for dh, dx, dy in second_group:
+        other = second_group.index((dh, dx, (YN - dy) % YN))
         source = part_two.at[lax.rem(x + dx, XN) * 4 + z // 2]
-        two.append(copy(source, got_two.at[other], (at(dx, 0, dy), lax.rem(b + db, BN))))
+        two.append(copy(source, got_two.at[other], (at(dx, 0, dy), lax.rem(half + dh, 2) * 2 + core)))
     for made in two:
         made.wait_recv()
     row_sum = part_two[x * 4 + z // 2]
-    for i in range(len(plane)):
+    for i in range(len(second_group)):
         row_sum = row_sum + got_two[i]
     offset = lax.rem(z, 2) * 64 + y * 16
-    gradient_out[...] = pltpu.roll(jnp.broadcast_to(row_sum, (8, TILE)), lax.rem(TILE - offset, TILE), 1)[0:1, :16] * scale
+    turned = pltpu.roll(jnp.broadcast_to(row_sum, (8, TILE)), lax.rem(TILE - offset, TILE), 1)
+    gradient_out[...] = turned[0:1, :16] * scale
 
     for made in started:
         made.wait_send()
@@ -297,15 +325,26 @@
         store.wait()
 
 
+def hand_on(focused, smoothed, gradient, focused_out, smoothed_out, gradient_out, held, row, sem):
+    moves = [
+        (src.at[q, pl.ds(h * 32, 32)], held.at[n, q, pl.ds(h * 32, 32)], dst.at[q, pl.ds(h * 32, 32)])
+        for n, (src, dst) in enumerate(((focused, focused_out), (smoothed, smoothed_out)))
+        for q in range(2)
+        for h in range(2)
+    ]
+    moves.append((gradient, row, gradient_out))
+    loads = [pltpu.make_async_copy(src, mid, sem.at[0, n]) for n, (src, mid, _) in enumerate(moves)]
+    stores = [pltpu.make_async_copy(mid, dst, sem.at[1, n]) for n, (_, mid, dst) in enumerate(moves)]
+    for made in loads:
+        made.start()
+    for made, store in zip(loads, stores):
+        made.wait()
+        store.start()
+    for made in stores:
+        made.wait()
+
+
 def shards(pulse_data, phase_error, steering, kernel_bank, tile_offsets, kernel_ids, counts):
-    w = lax.axis_index("wedge")
-    x, z, y = w // (ZN * YN), (w // YN) % ZN, w % YN
-    near = [w] + [x * 32 + z * 4 + (y + dy) % YN for dy in range(1, YN)] + [(w + 32) % 64]
-    rows = [lax.dynamic_index_in_dim(tile_offsets, k, 1, keepdims=False) for k in near]
-    ids = lax.dynamic_index_in_dim(kernel_ids, w, 1, keepdims=False)
-    live = lax.dynamic_index_in_dim(counts, w, 1, keepdims=False)
-    ids = jnp.where(jnp.arange(MAXB)[None, :] < live[:, None], ids, 8)
-    table = jnp.reshape(jnp.stack(rows + [ids]), (-1,))
     bf, f32 = jnp.bfloat16, jnp.float32
     block = pltpu.VMEM((8, 16, TILE), bf)
     scratch = [block] * 24
@@ -324,12 +363,19 @@
         pltpu.VMEM((2, 1, TILE), f32),
         pltpu.VMEM((2, 1, TILE), f32),
         pltpu.VMEM((8, 1, TILE), f32),
-        pltpu.VMEM((7, 8, 1, TILE), f32),
+        pltpu.VMEM((15, 8, 1, TILE), f32),
         pltpu.VMEM((8, 1, TILE), f32),
-        pltpu.VMEM((31, 1, TILE), f32),
+        pltpu.VMEM((15, 1, TILE), f32),
+        pltpu.VMEM((64, MAXB, 64), jnp.int32),
+        pltpu.VMEM((64, MAXB, 64), jnp.int32),
+        pltpu.VMEM((64, 64), jnp.int32),
+        pltpu.VMEM((1, 16), f32),
+        pltpu.VMEM((2, 16, 1024), bf),
+        pltpu.VMEM((8, 256), jnp.int32),
+        pltpu.SMEM((8, 256), jnp.int32),
         pltpu.SemaphoreType.DMA((COPIES,)),
         pltpu.SemaphoreType.DMA((COPIES,)),
-        pltpu.SemaphoreType.DMA((4,)),
+        pltpu.SemaphoreType.DMA((10,)),
     ]
     scale = math.sqrt(1024 / (4096 * 4096))
     image = jax.ShapeDtypeStruct((2, 64, 1024), f32)
@@ -338,20 +384,30 @@
     focused, smoothed, gradient = pl.pallas_call(
         functools.partial(kernel, scale),
         out_shape=(image, image, jax.ShapeDtypeStruct((1, 16), f32)),
-        in_specs=[pl.BlockSpec(memory_space=pltpu.SMEM), vmem, vmem, anywhere, anywhere],
+        in_specs=[anywhere] * 7,
         out_specs=(anywhere, anywhere, vmem),
         scratch_shapes=scratch,
         compiler_params=pltpu.CompilerParams(
-            collective_id=0, has_side_effects=True, vmem_limit_bytes=40 << 20
+            collective_id=0, has_side_effects=True, vmem_limit_bytes=62 << 20
         ),
     )(
-        table,
+        jnp.transpose(tile_offsets, (0, 2, 1)),
+        jnp.transpose(kernel_ids, (0, 2, 1)),
+        counts,
         jnp.reshape(phase_error, (1, 16)),
         pulse_data,
         jnp.reshape(steering, (128, 1024)),
         jnp.reshape(kernel_bank, (1024, 1024)),
     )
-    return focused, smoothed, jnp.reshape(gradient, (16,))
+    results = pl.pallas_call(
+        hand_on,
+        out_shape=(image, image, jax.ShapeDtypeStruct((1, 16), f32)),
+        in_specs=[anywhere] * 3,
+        out_specs=[anywhere] * 3,
+        scratch_shapes=[pltpu.VMEM((2, 2, 64, 1024), f32), pltpu.VMEM((1, 16), f32), pltpu.SemaphoreType.DMA((2, 9))],
+        compiler_params=pltpu.CompilerParams(vmem_limit_bytes=62 << 20),
+    )(focused, smoothed, gradient)
+    return results[0], results[1], jnp.reshape(results[2], (16,))
 
 
 def solution(mesh):

time: 64.3 us -> 57.4 us (0.89)
  local copies, waits for them, and re-layouts: 5.72 us -> 0 us
  Pallas kernels: 57.6 us -> 56.6 us
    pallas_call x1, Pallas kernels: 57.6 us -> 54.5 us  [shards(): pl.pallas_call(functools.partial(kernel, scale), out_shape=(image, image,...]
    unnamed x18 -> x0, local copies, waits for them, and re-layouts: 2.75 us -> none
    dynamic_slice x8 -> x0, local copies, waits for them, and re-layouts: 2.7 us -> none  [the longest x6 2.41 us: shards(): lax.dynamic_index_in_dim(tile_offsets, k, 1, keepdims=False)]
    pallas_call x0 -> x1, Pallas kernels: none -> 2.11 us  [shards(): pl.pallas_call(hand_on, out_shape=(image, image, jax.ShapeDtypeStruct((1,...]
where the time goes in v2:
time: 57.4 us; the launch traced here: 57.3 us
  Pallas kernels  56.6 us (99%)
  between operations  0.64 us (1%)
    pallas_call x1, Pallas kernels, shards(): pl.pallas_call(functools.partial(kernel, scale), out_shape=(image, image,...  54.5 us
    pallas_call x1, Pallas kernels, shards(): pl.pallas_call(hand_on, out_shape=(image, image, jax.ShapeDtypeStruct((1,...  2.11 us

profile of v2, /device:TPU:1, one launch (start us, length us, event | category | flops | bytes accessed | tf_op | source)
XLA Modules:
  0.0 57.3 jit_solution(4170760187205447105)
XLA Ops:
  0.6 54.5 %shard_map.94 = (f32[2,64,1024]{2,1,0:T(8,128)}, f32[2,64,1024]{2,1,0:T(8,128)}, f32[1,16]{1,0:T(1,128)}) custom-call(s32[64,4,64]{2,1,0:T(4,128)} %bitcast.8, s32[64,4,64]{2,1,0:T(4,128)} %bitcast.9, s32[64,64]{1,0:T(8,128)} %counts_in.1, f32[1,16]{1,0:T(1,128)} %bitcast.10, bf16[2,16,1024]{2,1,0:T(8,128)(2,1)} %pulses_in.1, bf16[128,1024]{1,0:T(8,128)(2,1)} %bitcast.7, ...), custom_call_target="tpu_custom_call" | custom-call | tf_op jit(solution)/shard_map/pallas_call | solution.py:384
  55.2 2.1 %shard_map.95 = (f32[2,64,1024]{2,1,0:T(8,128)}, f32[2,64,1024]{2,1,0:T(8,128)}, f32[1,16]{1,0:T(1,128)}) custom-call(f32[2,64,1024]{2,1,0:T(8,128)} %get-tuple-element.9.focused, f32[2,64,1024]{2,1,0:T(8,128)} %get-tuple-element.10.smoothed, f32[1,16]{1,0:T(1,128)} %get-tuple-element.11.gradient), custom_call_target="tpu_custom_call" | custom-call | tf_op jit(solution)/shard_map/pallas_call | solution.py:402

commit v3 on v2

--- a/solution.py
+++ b/solution.py
@@ -81,27 +81,33 @@
         return made
 
     ring = {}
-
-    def send_ring(stream, bufs, d):
-        up, down = (at(0, 1, 0), b), (at(0, ZN - 1, 0), b)
-        src_up, dst_up = bufs[(1 - d) % ZN], bufs[-d % ZN]
-        src_down, dst_down = bufs[d - 1], bufs[d]
-        if d == ZN // 2:
-            low = (slice(None),) * (len(dst_up.shape) - 4) + (pl.ds(0, 4),)
-            high = (slice(None),) * (len(dst_up.shape) - 4) + (pl.ds(4, 4),)
-            if len(dst_up.shape) == 3:
-                low, high = pl.ds(0, 4), pl.ds(4, 4)
-            else:
-                low, high = (slice(None), pl.ds(0, 4)), (slice(None), pl.ds(4, 4))
-            src_up, dst_up = src_up.at[low], dst_up.at[low]
-            src_down, dst_down = src_down.at[high], dst_down.at[high]
-        ring[stream, d] = (copy(src_up, dst_up, up), copy(src_down, dst_down, down))
-
-    def take_ring(stream, bufs, d):
-        for made in ring[stream, d]:
-            made.wait_recv()
-        if d < ZN // 2:
-            send_ring(stream, bufs, d + 1)
+    own0_ring = (own0, None)
+    own1_ring = (own1, None)
+    pair0_ring = (pair0, None)
+    column1_rings = [(column1, i) for i in range(YN - 1)]
+
+    def part(ref, index, half):
+        if index is None:
+            return ref if half is None else ref.at[half]
+        return ref.at[index] if half is None else ref.at[index, half]
+
+    def send_ring(name, d, sign):
+        bufs, index = name
+        key = (id(bufs), index)
+        half = None if d < ZN // 2 else pl.ds(0, 4) if sign > 0 else pl.ds(4, 4)
+        src = part(bufs[(-sign * (d - 1)) % ZN], index, half)
+        dst = part(bufs[(-sign * d) % ZN], index, half)
+        ring[key, d, sign] = copy(src, dst, (at(0, sign % ZN, 0), b))
+
+    def start_ring(name):
+        for sign in (1, -1):
+            send_ring(name, 1, sign)
+
+    def take_ring(name, d):
+        for sign in (1, -1):
+            ring[(id(name[0]), name[1]), d, sign].wait_recv()
+            if d < ZN // 2:
+                send_ring(name, d + 1, sign)
 
     def block_at(e, dx, dy):
         return at(dx, e, dy)
@@ -111,7 +117,7 @@
 
     y_copies, x_copies = {}, {}
 
-    def share(e):
+    def share_y(e):
         for dx, bufs in ((0, own0), (1, pair0)):
             k = block_at(e, dx, 0)
             for dy in range(1, YN):
@@ -120,12 +126,19 @@
         y_copies[e] = [
             copy(y_send[e].at[dy - 1], y_got[e].at[YN - dy - 1], (at(0, 0, dy), b)) for dy in range(1, YN)
         ]
-        for dy in range(YN):
+
+    def share_own(e):
+        k = block_at(e, 0, 0)
+        for j in range(MAXB):
+            x_send[e][0, j] = own1[e][pick(4, k, j)]
+        x_copies[e] = [copy(x_send[e].at[0], x_got[e].at[0], (at(1, 0, 0), b))]
+
+    def share_column(e):
+        for dy in range(1, YN):
             k = block_at(e, 0, dy)
             for j in range(MAXB):
-                t = pick(4, k, j)
-                x_send[e][dy, j] = own1[e][t] if dy == 0 else column1[e][dy - 1, t]
-        x_copies[e] = [copy(x_send[e], x_got[e], (at(1, 0, 0), b))]
+                x_send[e][dy, j] = column1[e][dy - 1, pick(4, k, j)]
+        x_copies[e] += [copy(x_send[e].at[pl.ds(1, 3)], x_got[e].at[pl.ds(1, 3)], (at(1, 0, 0), b))]
 
     def place(row, k, load):
         tiles = [load(j).astype(jnp.float32) for j in range(MAXB)]
@@ -181,9 +194,12 @@
         return [0] if d == 0 else [4] if d == 4 else [d, ZN - d]
 
     first_x = copy(own0[0], pair0[0], (at(1, 0, 0), b))
-    send_ring("own0", own0, 1)
-    first_y = [copy(own1[0], column1[0].at[YN - dy - 1], (at(0, 0, dy), b)) for dy in range(1, YN)]
-    send_ring("own1", own1, 1)
+    start_ring(own0_ring)
+    first_y = {
+        YN - dy - 1: copy(own1[0], column1[0].at[YN - dy - 1], (at(0, 0, dy), b)) for dy in (1, YN - 1)
+    }
+    start_ring(own1_ring)
+    first_y[1] = copy(own1[0], column1[0].at[1], (at(0, 0, 2), b))
 
     for made in index_loads:
         made.wait()
@@ -205,26 +221,39 @@
     table_v[...] = jnp.clip(picked, 0, 7)
     table_v[6:7, 0:wedges] = choose(counts, wedges)[6:7]
     load(table_v, table, 9).wait()
-    for turn in range(1, 6):
-        if turn <= 4:
-            take_ring("own0", own0, turn)
-            take_ring("own1", own1, turn)
-        if turn == 1:
-            first_x.wait_recv()
-            send_ring("pair0", pair0, 1)
-            for made in first_y:
-                made.wait_recv()
-            send_ring("column1", column1, 1)
-        else:
-            take_ring("pair0", pair0, turn - 1)
-            take_ring("column1", column1, turn - 1)
-        for e in slices(turn - 1):
-            share(e)
-        if turn == 2:
+    share_own(0)
+    first_x.wait_recv()
+    start_ring(pair0_ring)
+    take_ring(own0_ring, 1)
+    for i in (2, 0):
+        first_y[i].wait_recv()
+        start_ring(column1_rings[i])
+    share_y(0)
+    take_ring(own1_ring, 1)
+    for e in slices(1):
+        share_own(e)
+    first_y[1].wait_recv()
+    start_ring(column1_rings[1])
+    share_column(0)
+    for d in range(1, 5):
+        take_ring(pair0_ring, d)
+        if d < 4:
+            take_ring(own0_ring, d + 1)
+        for e in slices(d):
+            share_y(e)
+        for i in (2, 0):
+            take_ring(column1_rings[i], d)
+        if d < 4:
+            take_ring(own1_ring, d + 1)
+            for e in slices(d + 1):
+                share_own(e)
+        take_ring(column1_rings[1], d)
+        for e in slices(d):
+            share_column(e)
+        if d == 1:
             for made in loads:
                 made.wait()
-        if turn >= 2:
-            process(slices(turn - 2))
+        process(slices(d - 1))
     process(slices(4))
 
     steer = steer_v[...]
@@ -252,15 +281,17 @@
 
     squared = image[0] * image[0] + image[1] * image[1]
     cubed = jnp.concatenate([squared * image[0], squared * image[1]], axis=0).astype(jnp.bfloat16)
-    for n in range(8):
-        pulses_here = slice(n * 128, (n + 1) * 128)
-        late = slice(1024 + n * 128, 1024 + (n + 1) * 128)
+    for n in range(4):
+        pulses_here = slice(n * 256, (n + 1) * 256)
+        late = slice(1024 + n * 256, 1024 + (n + 1) * 256)
         by0 = lax.dot_general(cubed, resampled[pulses_here, :], across, preferred_element_type=jnp.float32)
         by1 = lax.dot_general(cubed, resampled[late, :], across, preferred_element_type=jnp.float32)
         s0 = steer_v[0:64, pulses_here].astype(jnp.float32)
         s1 = steer_v[64:128, pulses_here].astype(jnp.float32)
         terms = s0 * (by1[:64] - by0[64:]) + s1 * (by1[64:] + by0[:64])
-        part_one[n] = jnp.sum(terms, axis=0, keepdims=True)
+        summed = jnp.sum(terms, axis=0, keepdims=True)
+        part_one[2 * n] = summed[:, :TILE]
+        part_one[2 * n + 1] = summed[:, TILE:]
     core, half = lax.rem(b, 2), b // 2
     first_group = [(dz, dc) for dc in range(2) for dz in range(ZN) if (dz, dc) != (0, 0)]
     one = []

time: 57.4 us -> 55.2 us (0.962)
  Pallas kernels: 56.6 us -> 54.5 us
    pallas_call x1, Pallas kernels: 54.5 us -> 52.4 us  [shards(): pl.pallas_call(functools.partial(kernel, scale), out_shape=(image, image,...]
where the time goes in v3:
time: 55.2 us; the launch traced here: 55.1 us
  Pallas kernels  54.5 us (99%)
  between operations  0.64 us (1%)
    pallas_call x1, Pallas kernels, shards(): pl.pallas_call(functools.partial(kernel, scale), out_shape=(image, image,...  52.4 us
    pallas_call x1, Pallas kernels, shards(): pl.pallas_call(hand_on, out_shape=(image, image, jax.ShapeDtypeStruct((1,...  2.11 us

profile of v3, /device:TPU:1, one launch (start us, length us, event | category | flops | bytes accessed | tf_op | source)
XLA Modules:
  0.0 55.1 jit_solution(9040198399061950431)
XLA Ops:
  0.6 52.4 %shard_map.94 = (f32[2,64,1024]{2,1,0:T(8,128)}, f32[2,64,1024]{2,1,0:T(8,128)}, f32[1,16]{1,0:T(1,128)}) custom-call(s32[64,4,64]{2,1,0:T(4,128)} %bitcast.8, s32[64,4,64]{2,1,0:T(4,128)} %bitcast.9, s32[64,64]{1,0:T(8,128)} %counts_in.1, f32[1,16]{1,0:T(1,128)} %bitcast.10, bf16[2,16,1024]{2,1,0:T(8,128)(2,1)} %pulses_in.1, bf16[128,1024]{1,0:T(8,128)(2,1)} %bitcast.7, ...), custom_call_target="tpu_custom_call" | custom-call | tf_op jit(solution)/shard_map/pallas_call | solution.py:415
  53.0 2.1 %shard_map.95 = (f32[2,64,1024]{2,1,0:T(8,128)}, f32[2,64,1024]{2,1,0:T(8,128)}, f32[1,16]{1,0:T(1,128)}) custom-call(f32[2,64,1024]{2,1,0:T(8,128)} %get-tuple-element.9.focused, f32[2,64,1024]{2,1,0:T(8,128)} %get-tuple-element.10.smoothed, f32[1,16]{1,0:T(1,128)} %get-tuple-element.11.gradient), custom_call_target="tpu_custom_call" | custom-call | tf_op jit(solution)/shard_map/pallas_call | solution.py:433

commit v4 on v3

--- a/solution.py
+++ b/solution.py
@@ -24,7 +24,7 @@
     column1 = take(ZN)
     y_send, y_got = take(ZN), take(ZN)
     x_send, x_got = take(ZN), take(ZN)
-    lhs, resampled, bank_v, steer_v, image, smooth = take(6)
+    lhs, resampled, bank_v, steer_v, steer_r, steer_a, steer_b, image, smooth = take(9)
     rows_send, rows_got, cols_send, cols_got = take(4)
     part_one, got_one, part_two, got_two = take(4)
     offsets, ids, counts, phase, pulses, table_v, table = take(7)
@@ -140,55 +140,73 @@
                 x_send[e][dy, j] = column1[e][dy - 1, pick(4, k, j)]
         x_copies[e] += [copy(x_send[e].at[pl.ds(1, 3)], x_got[e].at[pl.ds(1, 3)], (at(1, 0, 0), b))]
 
-    def place(row, k, load):
-        tiles = [load(j).astype(jnp.float32) for j in range(MAXB)]
+    def place(row, k, loads_of):
         names = [jnp.where(j < table[6, k], pick(5, k, j), 8) for j in range(MAXB)]
-        row = pl.multiple_of(row, 16)
-        for m in range(8):
-            total = jnp.zeros((16, TILE), jnp.float32)
-            for j in range(MAXB):
-                total = total + jnp.where(names[j] == m, tiles[j], 0.0)
-            lhs[pl.ds(row, 16), m * TILE : (m + 1) * TILE] = total.astype(jnp.bfloat16)
-
-    def process(es):
-        for index, e in enumerate(es):
-            for made in y_copies[e] + x_copies[e]:
-                made.wait_recv()
-
-            def row_of(q, dx, dy, index=index):
-                return index * 256 + q * 128 + lax.rem(x + dx, XN) * 64 + lax.rem(y + dy, YN) * 16
-
-            for dx, bufs in ((0, own0), (1, pair0)):
-                k = block_at(e, dx, 0)
-                place(row_of(0, dx, 0), k, lambda j: bufs[e][pick(0, k, j)])
-            k = block_at(e, 0, 0)
-            place(row_of(1, 0, 0), k, lambda j: own1[e][pick(0, k, j)])
-
-            @pl.loop(1, YN)
-            def _(dy, e=e, row_of=row_of):
-                for dx in range(XN):
-                    k = block_at(e, dx, dy)
-                    place(row_of(0, dx, dy), k, lambda j: y_got[e][dy - 1, dx, j])
-                k = block_at(e, 0, dy)
-                place(row_of(1, 0, dy), k, lambda j: column1[e][dy - 1, pick(0, k, j)])
-
-            @pl.loop(0, YN)
-            def _(dy, e=e, row_of=row_of):
-                k = block_at(e, 1, dy)
-                place(row_of(1, 1, dy), k, lambda j: x_got[e][dy, j])
-
-        @pl.loop(0, 4)
+        for q, load_tile in enumerate(loads_of):
+            tiles = [load_tile(j).astype(jnp.float32) for j in range(MAXB)]
+            summed = []
+            for i in range(MAXB):
+                total = tiles[i]
+                for j in range(i + 1, MAXB):
+                    total = total + jnp.where(names[i] == names[j], tiles[j], 0.0)
+                summed.append(total.astype(jnp.bfloat16))
+            here = pl.multiple_of(q * 128 + row, 16)
+            for m in range(8):
+                value = jnp.zeros((16, TILE), jnp.bfloat16)
+                for j in reversed(range(MAXB)):
+                    value = jnp.where(names[j] == m, summed[j], value)
+                lhs[pl.ds(here, 16), m * TILE : (m + 1) * TILE] = value
+
+    turns = [0, 7, 1, 6, 2, 5, 3, 4]
+
+    def process(e):
+        for made in y_copies[e] + x_copies[e]:
+            made.wait_recv()
+
+        def row_of(dx, dy):
+            return lax.rem(x + dx, XN) * 64 + lax.rem(y + dy, YN) * 16
+
+        k0, k1 = block_at(e, 0, 0), block_at(e, 1, 0)
+        place(
+            row_of(0, 0),
+            k0,
+            [lambda j: own0[e][pick(0, k0, j)], lambda j: own1[e][pick(0, k0, j)]],
+        )
+        place(row_of(1, 0), k1, [lambda j: pair0[e][pick(0, k1, j)], lambda j: x_got[e][0, j]])
+
+        @pl.loop(1, YN)
+        def _(dy):
+            near, far = block_at(e, 0, dy), block_at(e, 1, dy)
+            place(
+                row_of(0, dy),
+                near,
+                [lambda j: y_got[e][dy - 1, 0, j], lambda j: column1[e][dy - 1, pick(0, near, j)]],
+            )
+            place(row_of(1, dy), far, [lambda j: y_got[e][dy - 1, 1, j], lambda j: x_got[e][dy, j]])
+
+        place_at = turns.index(e) * 128
+
+        @pl.loop(0, 2)
         def _(n):
-            columns = pl.ds(pl.multiple_of(n * 256, 256), 256)
-            rows = 256 * len(es)
-            got = jnp.dot(lhs[0:rows, :], bank_v[:, columns], preferred_element_type=jnp.float32)
+            columns = pl.ds(pl.multiple_of(n * 512, 512), 512)
+            got = jnp.dot(lhs[...], bank_v[:, columns], preferred_element_type=jnp.float32)
             got = got.astype(jnp.bfloat16)
-            for index, e in enumerate(es):
-                for q in range(2):
-                    for xa in range(XN):
-                        start = q * 1024 + xa * 512 + lax.rem(z + e, ZN) * 64
-                        here = index * 256 + q * 128 + xa * 64
-                        resampled[pl.ds(pl.multiple_of(start, 64), 64), columns] = got[here : here + 64]
+            resampled[place_at : place_at + 128, columns] = got[:128]
+            resampled[1024 + place_at : 1024 + place_at + 128, columns] = got[128:]
+
+    def focus(first, last):
+        inner = slice(first * 128, last * 128)
+        late = slice(1024 + first * 128, 1024 + last * 128)
+
+        for n in range(2):
+            columns = slice(n * 512, (n + 1) * 512)
+            by_real = jnp.dot(steer_r[:, inner], resampled[inner, columns], preferred_element_type=jnp.float32)
+            by_imag = jnp.dot(steer_r[:, inner], resampled[late, columns], preferred_element_type=jnp.float32)
+            real, imag = by_real[:64] - by_imag[64:], by_imag[:64] + by_real[64:]
+            if first:
+                real, imag = real + image[0, :, columns], imag + image[1, :, columns]
+            image[0, :, columns] = real
+            image[1, :, columns] = imag
 
     def slices(d):
         return [0] if d == 0 else [4] if d == 4 else [d, ZN - d]
@@ -220,7 +238,8 @@
     picked = jnp.where(row == 5, choose(ids, wedges * MAXB), choose(offsets, wedges * MAXB))
     table_v[...] = jnp.clip(picked, 0, 7)
     table_v[6:7, 0:wedges] = choose(counts, wedges)[6:7]
-    load(table_v, table, 9).wait()
+    table_load = load(table_v, table, 9)
+    table_load.wait()
     share_own(0)
     first_x.wait_recv()
     start_ring(pair0_ring)
@@ -235,12 +254,31 @@
     first_y[1].wait_recv()
     start_ring(column1_rings[1])
     share_column(0)
+
+    loads[1].wait()
+    low_half = lax.broadcasted_iota(jnp.int32, (128, TILE), 1) < 64
+    for n, e in enumerate(turns):
+        zz = lax.rem(z + e, ZN)
+        odd = lax.rem(zz, 2)
+        pieces = []
+        for xx in range(XN):
+            columns = pl.ds(pl.multiple_of((xx * 4 + zz // 2) * TILE, TILE), TILE)
+            turn = lax.rem(odd + xx, 2) * 64
+            pieces.append(pltpu.roll(steer_v[:, columns].astype(jnp.float32), turn, 1))
+        piece = jnp.where(low_half, pieces[0], pieces[1])
+        here = slice(n * TILE, (n + 1) * TILE)
+        steer_r[:, here] = piece.astype(jnp.bfloat16)
+        steer_a[here, :] = jnp.transpose(piece)
+        steer_b[here, :] = jnp.transpose(jnp.concatenate([piece[64:], -piece[:64]], axis=0))
+
     for d in range(1, 5):
         take_ring(pair0_ring, d)
         if d < 4:
             take_ring(own0_ring, d + 1)
         for e in slices(d):
             share_y(e)
+        if d >= 3:
+            process(d - 2)
         for i in (2, 0):
             take_ring(column1_rings[i], d)
         if d < 4:
@@ -251,18 +289,14 @@
         for e in slices(d):
             share_column(e)
         if d == 1:
-            for made in loads:
-                made.wait()
-        process(slices(d - 1))
-    process(slices(4))
-
-    steer = steer_v[...]
-    for n in range(4):
-        columns = slice(n * 256, (n + 1) * 256)
-        by_real = jnp.dot(steer, resampled[0:1024, columns], preferred_element_type=jnp.float32)
-        by_imag = jnp.dot(steer, resampled[1024:2048, columns], preferred_element_type=jnp.float32)
-        image[0, :, columns] = by_real[:64] - by_imag[64:]
-        image[1, :, columns] = by_imag[:64] + by_real[64:]
+            loads[0].wait()
+        if d == 4:
+            focus(0, 5)
+        process((ZN - (d - 1)) % ZN)
+    process(3)
+    focus(5, 7)
+    process(4)
+    focus(7, 8)
     stores = [pltpu.make_async_copy(image, focused_out, load_sem.at[2])]
     stores[0].start()
 
@@ -282,22 +316,20 @@
     squared = image[0] * image[0] + image[1] * image[1]
     cubed = jnp.concatenate([squared * image[0], squared * image[1]], axis=0).astype(jnp.bfloat16)
     for n in range(4):
-        pulses_here = slice(n * 256, (n + 1) * 256)
+        inner = slice(n * 256, (n + 1) * 256)
         late = slice(1024 + n * 256, 1024 + (n + 1) * 256)
-        by0 = lax.dot_general(cubed, resampled[pulses_here, :], across, preferred_element_type=jnp.float32)
-        by1 = lax.dot_general(cubed, resampled[late, :], across, preferred_element_type=jnp.float32)
-        s0 = steer_v[0:64, pulses_here].astype(jnp.float32)
-        s1 = steer_v[64:128, pulses_here].astype(jnp.float32)
-        terms = s0 * (by1[:64] - by0[64:]) + s1 * (by1[64:] + by0[:64])
-        summed = jnp.sum(terms, axis=0, keepdims=True)
-        part_one[2 * n] = summed[:, :TILE]
-        part_one[2 * n + 1] = summed[:, TILE:]
+        by0 = lax.dot_general(resampled[inner, :], cubed, across, preferred_element_type=jnp.float32)
+        by1 = lax.dot_general(resampled[late, :], cubed, across, preferred_element_type=jnp.float32)
+        terms = jnp.sum(steer_a[inner, :] * by1 + steer_b[inner, :] * by0, axis=1, keepdims=True)
+        for h in range(2):
+            part = jnp.where(eye, terms[h * TILE : (h + 1) * TILE], 0.0)
+            part_one[2 * n + h] = jnp.sum(part, axis=0, keepdims=True)
     core, half = lax.rem(b, 2), b // 2
     first_group = [(dz, dc) for dc in range(2) for dz in range(ZN) if (dz, dc) != (0, 0)]
     one = []
     for dz, dc in first_group:
         other = first_group.index(((ZN - dz) % ZN, dc))
-        one.append(copy(part_one, got_one.at[other], (at(0, dz, 0), half * 2 + lax.rem(core + dc, 2))))
+        one.append(copy(part_one.at[turns.index(dz)], got_one.at[other], (at(0, dz, 0), half * 2 + lax.rem(core + dc, 2))))
 
     for made in edge:
         made.wait_recv()
@@ -331,7 +363,7 @@
 
     for made in one:
         made.wait_recv()
-    total = part_one[...]
+    total = part_one[turns.index(0)]
     for i in range(len(first_group)):
         total = total + got_one[i]
     part_two[...] = total
@@ -339,14 +371,13 @@
     two = []
     for dh, dx, dy in second_group:
         other = second_group.index((dh, dx, (YN - dy) % YN))
-        source = part_two.at[lax.rem(x + dx, XN) * 4 + z // 2]
-        two.append(copy(source, got_two.at[other], (at(dx, 0, dy), lax.rem(half + dh, 2) * 2 + core)))
+        two.append(copy(part_two, got_two.at[other], (at(dx, 0, dy), lax.rem(half + dh, 2) * 2 + core)))
     for made in two:
         made.wait_recv()
-    row_sum = part_two[x * 4 + z // 2]
+    row_sum = part_two[...]
     for i in range(len(second_group)):
         row_sum = row_sum + got_two[i]
-    offset = lax.rem(z, 2) * 64 + y * 16
+    offset = x * 64 + y * 16
     turned = pltpu.roll(jnp.broadcast_to(row_sum, (8, TILE)), lax.rem(TILE - offset, TILE), 1)
     gradient_out[...] = turned[0:1, :16] * scale
 
@@ -383,10 +414,13 @@
     scratch += [pltpu.VMEM((3, 2, 4, 16, TILE), bf)] * 16
     scratch += [pltpu.VMEM((4, 4, 16, TILE), bf)] * 16
     scratch += [
-        pltpu.VMEM((512, 1024), bf),
+        pltpu.VMEM((256, 1024), bf),
         pltpu.VMEM((2048, 1024), bf),
         pltpu.VMEM((1024, 1024), bf),
         pltpu.VMEM((128, 1024), bf),
+        pltpu.VMEM((128, 1024), bf),
+        pltpu.VMEM((1024, TILE), f32),
+        pltpu.VMEM((1024, TILE), f32),
         pltpu.VMEM((2, 64, 1024), f32),
         pltpu.VMEM((2, 64, 1024), f32),
         pltpu.VMEM((2, 2, 1024), f32),
@@ -394,8 +428,8 @@
         pltpu.VMEM((2, 1, TILE), f32),
         pltpu.VMEM((2, 1, TILE), f32),
         pltpu.VMEM((8, 1, TILE), f32),
-        pltpu.VMEM((15, 8, 1, TILE), f32),
-        pltpu.VMEM((8, 1, TILE), f32),
+        pltpu.VMEM((15, 1, TILE), f32),
+        pltpu.VMEM((1, TILE), f32),
         pltpu.VMEM((15, 1, TILE), f32),
         pltpu.VMEM((64, MAXB, 64), jnp.int32),
         pltpu.VMEM((64, MAXB, 64), jnp.int32),

time: 55.2 us -> 53.6 us (0.971)
  Pallas kernels: 54.5 us -> 52.8 us
    pallas_call x1, Pallas kernels: 52.4 us -> 50.7 us  [shards(): pl.pallas_call(functools.partial(kernel, scale), out_shape=(image, image,...]
where the time goes in v4:
time: 53.6 us; the launch traced here: 53.5 us
  Pallas kernels  52.8 us (99%)
  between operations  0.64 us (1%)
    pallas_call x1, Pallas kernels, shards(): pl.pallas_call(functools.partial(kernel, scale), out_shape=(image, image,...  50.7 us
    pallas_call x1, Pallas kernels, shards(): pl.pallas_call(hand_on, out_shape=(image, image, jax.ShapeDtypeStruct((1,...  2.11 us

profile of v4, /device:TPU:1, one launch (start us, length us, event | category | flops | bytes accessed | tf_op | source)
XLA Modules:
  0.0 53.5 jit_solution(5017237398127340086)
XLA Ops:
  0.6 50.7 %shard_map.94 = (f32[2,64,1024]{2,1,0:T(8,128)}, f32[2,64,1024]{2,1,0:T(8,128)}, f32[1,16]{1,0:T(1,128)}) custom-call(s32[64,4,64]{2,1,0:T(4,128)} %bitcast.8, s32[64,4,64]{2,1,0:T(4,128)} %bitcast.9, s32[64,64]{1,0:T(8,128)} %counts_in.1, f32[1,16]{1,0:T(1,128)} %bitcast.10, bf16[2,16,1024]{2,1,0:T(8,128)(2,1)} %pulses_in.1, bf16[128,1024]{1,0:T(8,128)(2,1)} %bitcast.7, ...), custom_call_target="tpu_custom_call" | custom-call | tf_op jit(solution)/shard_map/pallas_call | solution.py:449
  51.4 2.1 %shard_map.95 = (f32[2,64,1024]{2,1,0:T(8,128)}, f32[2,64,1024]{2,1,0:T(8,128)}, f32[1,16]{1,0:T(1,128)}) custom-call(f32[2,64,1024]{2,1,0:T(8,128)} %get-tuple-element.9.focused, f32[2,64,1024]{2,1,0:T(8,128)} %get-tuple-element.10.smoothed, f32[1,16]{1,0:T(1,128)} %get-tuple-element.11.gradient), custom_call_target="tpu_custom_call" | custom-call | tf_op jit(solution)/shard_map/pallas_call | solution.py:467

commit v5 on v4

--- a/solution.py
+++ b/solution.py
@@ -24,7 +24,7 @@
     column1 = take(ZN)
     y_send, y_got = take(ZN), take(ZN)
     x_send, x_got = take(ZN), take(ZN)
-    lhs, resampled, bank_v, steer_v, steer_r, steer_a, steer_b, image, smooth = take(9)
+    lhs_a, lhs_b, resampled, bank_v, steer_v, steer_r, steer_a, steer_b, image, smooth = take(10)
     rows_send, rows_got, cols_send, cols_got = take(4)
     part_one, got_one, part_two, got_two = take(4)
     offsets, ids, counts, phase, pulses, table_v, table = take(7)
@@ -140,9 +140,9 @@
                 x_send[e][dy, j] = column1[e][dy - 1, pick(4, k, j)]
         x_copies[e] += [copy(x_send[e].at[pl.ds(1, 3)], x_got[e].at[pl.ds(1, 3)], (at(1, 0, 0), b))]
 
-    def place(row, k, loads_of):
+    def place(lhs, row, k, loads_of):
         names = [jnp.where(j < table[6, k], pick(5, k, j), 8) for j in range(MAXB)]
-        for q, load_tile in enumerate(loads_of):
+        for q, load_tile in loads_of:
             tiles = [load_tile(j).astype(jnp.float32) for j in range(MAXB)]
             summed = []
             for i in range(MAXB):
@@ -159,40 +159,57 @@
 
     turns = [0, 7, 1, 6, 2, 5, 3, 4]
 
-    def process(e):
-        for made in y_copies[e] + x_copies[e]:
-            made.wait_recv()
-
-        def row_of(dx, dy):
-            return lax.rem(x + dx, XN) * 64 + lax.rem(y + dy, YN) * 16
-
-        k0, k1 = block_at(e, 0, 0), block_at(e, 1, 0)
-        place(
-            row_of(0, 0),
-            k0,
-            [lambda j: own0[e][pick(0, k0, j)], lambda j: own1[e][pick(0, k0, j)]],
-        )
-        place(row_of(1, 0), k1, [lambda j: pair0[e][pick(0, k1, j)], lambda j: x_got[e][0, j]])
-
-        @pl.loop(1, YN)
-        def _(dy):
-            near, far = block_at(e, 0, dy), block_at(e, 1, dy)
-            place(
-                row_of(0, dy),
-                near,
-                [lambda j: y_got[e][dy - 1, 0, j], lambda j: column1[e][dy - 1, pick(0, near, j)]],
-            )
-            place(row_of(1, dy), far, [lambda j: y_got[e][dy - 1, 1, j], lambda j: x_got[e][dy, j]])
-
+    def arrived(made):
+        for one in made:
+            one.wait_recv()
+
+    def near_places(e, lhs, dx, dy):
+        row = lax.rem(x + dx, XN) * 64 + lax.rem(y + dy, YN) * 16
+        k = block_at(e, dx, dy)
+        if dx == 0 and dy == 0:
+            loads_of = [(0, lambda j: own0[e][pick(0, k, j)]), (1, lambda j: own1[e][pick(0, k, j)])]
+        elif dx == 0:
+            loads_of = [
+                (0, lambda j: y_got[e][dy - 1, 0, j]),
+                (1, lambda j: column1[e][dy - 1, pick(0, k, j)]),
+            ]
+        elif dy == 0:
+            loads_of = [(0, lambda j: pair0[e][pick(0, k, j)]), (1, lambda j: x_got[e][0, j])]
+        else:
+            loads_of = [(0, lambda j: y_got[e][dy - 1, 1, j]), (1, lambda j: x_got[e][dy, j])]
+        return lhs, row, k, loads_of
+
+    def far_last(e, lhs):
+        early, late = [], []
+        for dx in range(XN):
+            for dy in range(YN):
+                lhs, row, k, loads_of = near_places(e, lhs, dx, dy)
+                early.append((lhs, row, k, loads_of if dx == 0 else loads_of[:1]))
+                if dx == 1:
+                    late.append((lhs, row, k, loads_of[1:]))
+        return early, late
+
+    def places(e, lhs):
+        return [near_places(e, lhs, dx, dy) for dx in range(XN) for dy in range(YN)]
+
+    def product(e, lhs, beside=()):
         place_at = turns.index(e) * 128
-
-        @pl.loop(0, 2)
-        def _(n):
-            columns = pl.ds(pl.multiple_of(n * 512, 512), 512)
+        share = -(-len(beside) // 2)
+        for n in range(2):
+            columns = slice(n * 512, (n + 1) * 512)
             got = jnp.dot(lhs[...], bank_v[:, columns], preferred_element_type=jnp.float32)
             got = got.astype(jnp.bfloat16)
             resampled[place_at : place_at + 128, columns] = got[:128]
             resampled[1024 + place_at : 1024 + place_at + 128, columns] = got[128:]
+            for item in beside[n * share : (n + 1) * share]:
+                place(*item)
+
+    held = lhs_a, lhs_b
+
+    def step(position):
+        e, following = turns[position], turns[position + 1]
+        arrived(y_copies[following] + x_copies[following])
+        product(e, held[position % 2], places(following, held[(position + 1) % 2]))
 
     def focus(first, last):
         inner = slice(first * 128, last * 128)
@@ -278,7 +295,7 @@
         for e in slices(d):
             share_y(e)
         if d >= 3:
-            process(d - 2)
+            step(2 * d - 5)
         for i in (2, 0):
             take_ring(column1_rings[i], d)
         if d < 4:
@@ -290,12 +307,22 @@
             share_column(e)
         if d == 1:
             loads[0].wait()
-        if d == 4:
-            focus(0, 5)
-        process((ZN - (d - 1)) % ZN)
-    process(3)
+        if d == 1:
+            arrived(y_copies[0] + x_copies[0])
+            for item in places(0, held[0]):
+                place(*item)
+        else:
+            step(2 * d - 4)
+    focus(0, 5)
+    step(5)
+    arrived(y_copies[4])
+    early, late = far_last(4, held[1])
+    product(3, held[0], early)
     focus(5, 7)
-    process(4)
+    arrived(x_copies[4])
+    for item in late:
+        place(*item)
+    product(4, held[1])
     focus(7, 8)
     stores = [pltpu.make_async_copy(image, focused_out, load_sem.at[2])]
     stores[0].start()
@@ -414,6 +441,7 @@
     scratch += [pltpu.VMEM((3, 2, 4, 16, TILE), bf)] * 16
     scratch += [pltpu.VMEM((4, 4, 16, TILE), bf)] * 16
     scratch += [
+        pltpu.VMEM((256, 1024), bf),
         pltpu.VMEM((256, 1024), bf),
         pltpu.VMEM((2048, 1024), bf),
         pltpu.VMEM((1024, 1024), bf),

time: 53.6 us -> 51.7 us (0.965)
  Pallas kernels: 52.8 us -> 50.9 us
    pallas_call x1, Pallas kernels: 50.7 us -> 48.8 us  [shards(): pl.pallas_call(functools.partial(kernel, scale), out_shape=(image, image,...]
where the time goes in v5:
time: 51.7 us; the launch traced here: 51.6 us
  Pallas kernels  50.9 us (98%)
  between operations  0.64 us (1%)
    pallas_call x1, Pallas kernels, shards(): pl.pallas_call(functools.partial(kernel, scale), out_shape=(image, image,...  48.8 us
    pallas_call x1, Pallas kernels, shards(): pl.pallas_call(hand_on, out_shape=(image, image, jax.ShapeDtypeStruct((1,...  2.11 us

profile of v5, /device:TPU:1, one launch (start us, length us, event | category | flops | bytes accessed | tf_op | source)
XLA Modules:
  0.0 51.6 jit_solution(14018914445263433474)
XLA Ops:
  0.6 48.8 %shard_map.94 = (f32[2,64,1024]{2,1,0:T(8,128)}, f32[2,64,1024]{2,1,0:T(8,128)}, f32[1,16]{1,0:T(1,128)}) custom-call(s32[64,4,64]{2,1,0:T(4,128)} %bitcast.8, s32[64,4,64]{2,1,0:T(4,128)} %bitcast.9, s32[64,64]{1,0:T(8,128)} %counts_in.1, f32[1,16]{1,0:T(1,128)} %bitcast.10, bf16[2,16,1024]{2,1,0:T(8,128)(2,1)} %pulses_in.1, bf16[128,1024]{1,0:T(8,128)(2,1)} %bitcast.7, ...), custom_call_target="tpu_custom_call" | custom-call | tf_op jit(solution)/shard_map/pallas_call | solution.py:477
  49.5 2.1 %shard_map.95 = (f32[2,64,1024]{2,1,0:T(8,128)}, f32[2,64,1024]{2,1,0:T(8,128)}, f32[1,16]{1,0:T(1,128)}) custom-call(f32[2,64,1024]{2,1,0:T(8,128)} %get-tuple-element.9.focused, f32[2,64,1024]{2,1,0:T(8,128)} %get-tuple-element.10.smoothed, f32[1,16]{1,0:T(1,128)} %get-tuple-element.11.gradient), custom_call_target="tpu_custom_call" | custom-call | tf_op jit(solution)/shard_map/pallas_call | solution.py:495

commit v6 on v5

--- a/solution.py
+++ b/solution.py
@@ -256,14 +256,14 @@
     table_v[...] = jnp.clip(picked, 0, 7)
     table_v[6:7, 0:wedges] = choose(counts, wedges)[6:7]
     table_load = load(table_v, table, 9)
-    table_load.wait()
-    share_own(0)
     first_x.wait_recv()
     start_ring(pair0_ring)
     take_ring(own0_ring, 1)
     for i in (2, 0):
         first_y[i].wait_recv()
         start_ring(column1_rings[i])
+    table_load.wait()
+    share_own(0)
     share_y(0)
     take_ring(own1_ring, 1)
     for e in slices(1):

time: 51.7 us -> 51.7 us (level)
  no operation moved by 1% of the time
where the time goes in v6:
time: 51.7 us; the launch traced here: 51.6 us
  Pallas kernels  51 us (99%)
  between operations  0.64 us (1%)
    pallas_call x1, Pallas kernels, shards(): pl.pallas_call(functools.partial(kernel, scale), out_shape=(image, image,...  48.8 us
    pallas_call x1, Pallas kernels, shards(): pl.pallas_call(hand_on, out_shape=(image, image, jax.ShapeDtypeStruct((1,...  2.11 us

profile of v6, /device:TPU:1, one launch (start us, length us, event | category | flops | bytes accessed | tf_op | source)
XLA Modules:
  0.0 51.6 jit_solution(17631827991761909155)
XLA Ops:
  0.6 48.8 %shard_map.94 = (f32[2,64,1024]{2,1,0:T(8,128)}, f32[2,64,1024]{2,1,0:T(8,128)}, f32[1,16]{1,0:T(1,128)}) custom-call(s32[64,4,64]{2,1,0:T(4,128)} %bitcast.8, s32[64,4,64]{2,1,0:T(4,128)} %bitcast.9, s32[64,64]{1,0:T(8,128)} %counts_in.1, f32[1,16]{1,0:T(1,128)} %bitcast.10, bf16[2,16,1024]{2,1,0:T(8,128)(2,1)} %pulses_in.1, bf16[128,1024]{1,0:T(8,128)(2,1)} %bitcast.7, ...), custom_call_target="tpu_custom_call" | custom-call | tf_op jit(solution)/shard_map/pallas_call | solution.py:477
  49.5 2.1 %shard_map.95 = (f32[2,64,1024]{2,1,0:T(8,128)}, f32[2,64,1024]{2,1,0:T(8,128)}, f32[1,16]{1,0:T(1,128)}) custom-call(f32[2,64,1024]{2,1,0:T(8,128)} %get-tuple-element.9.focused, f32[2,64,1024]{2,1,0:T(8,128)} %get-tuple-element.10.smoothed, f32[1,16]{1,0:T(1,128)} %get-tuple-element.11.gradient), custom_call_target="tpu_custom_call" | custom-call | tf_op jit(solution)/shard_map/pallas_call | solution.py:495

commit v7 on v6

--- a/solution.py
+++ b/solution.py
@@ -388,6 +388,8 @@
     stores.append(pltpu.make_async_copy(smooth, smoothed_out, load_sem.at[3]))
     stores[1].start()
 
+    for made in started:
+        made.wait_send()
     for made in one:
         made.wait_recv()
     total = part_one[turns.index(0)]
@@ -399,6 +401,10 @@
     for dh, dx, dy in second_group:
         other = second_group.index((dh, dx, (YN - dy) % YN))
         two.append(copy(part_two, got_two.at[other], (at(dx, 0, dy), lax.rem(half + dh, 2) * 2 + core)))
+    for store in stores:
+        store.wait()
+    for made in two:
+        made.wait_send()
     for made in two:
         made.wait_recv()
     row_sum = part_two[...]
@@ -407,11 +413,6 @@
     offset = x * 64 + y * 16
     turned = pltpu.roll(jnp.broadcast_to(row_sum, (8, TILE)), lax.rem(TILE - offset, TILE), 1)
     gradient_out[...] = turned[0:1, :16] * scale
-
-    for made in started:
-        made.wait_send()
-    for store in stores:
-        store.wait()
 
 
 def hand_on(focused, smoothed, gradient, focused_out, smoothed_out, gradient_out, held, row, sem):

time: 51.7 us -> 51.5 us (level)
  no operation moved by 1% of the time
where the time goes in v7:
time: 51.5 us; the launch traced here: 51.4 us
  Pallas kernels  50.7 us (98%)
  between operations  0.64 us (1%)
    pallas_call x1, Pallas kernels, shards(): pl.pallas_call(functools.partial(kernel, scale), out_shape=(image, image,...  48.6 us
    pallas_call x1, Pallas kernels, shards(): pl.pallas_call(hand_on, out_shape=(image, image, jax.ShapeDtypeStruct((1,...  2.11 us

profile of v7, /device:TPU:1, one launch (start us, length us, event | category | flops | bytes accessed | tf_op | source)
XLA Modules:
  0.0 51.4 jit_solution(8582584609445279577)
XLA Ops:
  0.6 48.6 %shard_map.94 = (f32[2,64,1024]{2,1,0:T(8,128)}, f32[2,64,1024]{2,1,0:T(8,128)}, f32[1,16]{1,0:T(1,128)}) custom-call(s32[64,4,64]{2,1,0:T(4,128)} %bitcast.8, s32[64,4,64]{2,1,0:T(4,128)} %bitcast.9, s32[64,64]{1,0:T(8,128)} %counts_in.1, f32[1,16]{1,0:T(1,128)} %bitcast.10, bf16[2,16,1024]{2,1,0:T(8,128)(2,1)} %pulses_in.1, bf16[128,1024]{1,0:T(8,128)(2,1)} %bitcast.7, ...), custom_call_target="tpu_custom_call" | custom-call | tf_op jit(solution)/shard_map/pallas_call | solution.py:478
  49.3 2.1 %shard_map.95 = (f32[2,64,1024]{2,1,0:T(8,128)}, f32[2,64,1024]{2,1,0:T(8,128)}, f32[1,16]{1,0:T(1,128)}) custom-call(f32[2,64,1024]{2,1,0:T(8,128)} %get-tuple-element.9.focused, f32[2,64,1024]{2,1,0:T(8,128)} %get-tuple-element.10.smoothed, f32[1,16]{1,0:T(1,128)} %get-tuple-element.11.gradient), custom_call_target="tpu_custom_call" | custom-call | tf_op jit(solution)/shard_map/pallas_call | solution.py:496
